TPU v7x, 128 devices: a whole 4x4x4 slice. The times are simulated.
128 devices in a mesh: seq: 16 (over y, z), tp: 8 (over x, core).
Axes of the slice: x: 4, y: 4, z: 4, core: 2. Of those that a mesh axis runs over, the one named last changes fastest.
Arguments:
- q_raw: bfloat16 [2048, 8192], P('seq', 'tp'), may hold values from -80 to 80
- out_grad: bfloat16 [2048, 8192], P('seq', 'tp'), may hold values from -384 to 384
- q_gain: float32 [128], replicated, may hold values from 0.1 to 1.9
- image_keys: bfloat16 [16, 6404, 1024], P('seq', None, 'tp'), may hold values from -130 to 130
- image_values: bfloat16 [16, 6404, 1024], P('seq', None, 'tp'), may hold values from -6 to 6
- block_images: int32 [16, 2], replicated, may hold values from -1 to 15, as said below
- image_slot: int32 [16], replicated, may hold values from 0 to 15, as said below
- tile_counts: int32 [16], replicated, may hold values from 1 to 4, as said below
- q_weight: bfloat16 [8192, 8192], P(None, 'tp'), may hold values from -0.0625 to 0.0625
Outputs:
- text_grad: bfloat16 [2048, 8192], P(('seq', 'tp'))
- key_grad: bfloat16 [16, 6404, 1024], P('seq', None, 'tp')
- value_grad: bfloat16 [16, 6404, 1024], P('seq', None, 'tp')
Inputs may be any that keep to these rules, and one draw needn't show every extreme that they name: `block_images`: entry 0 over all blocks is a permutation of the image ids. Entry 1 of block 0 is -1, and entry 1 of block b is entry 0 of block b - 1 for b >= 1, so that at most 2 blocks read one image. A permutation: image i is held in row image_slot[i] of image_keys and image_values; that row lies on index image_slot[i] // 1 of seq, the index that holds the text block whose entry 0 is i. Image i uses its first tile_counts[i] * 1601 key rows; the rest are padding that no query reads. Some image has 4 tiles and some has one.
All inputs are finite; a program needn't handle non-finite values.
Results may differ from a plain program's by a relative error of at most 0.02.
The roundings to bfloat16 on the way count: a program that leaves them out, or rounds other values in their place, can miss the bound.
Values may be sent and summed in bfloat16 or wider, within the bound.
A program may use at most 128 MiB of HBM per device.

v0:
```python
from functools import partial
import math

import jax
import jax.numpy as jnp
from jax import lax
from jax.sharding import PartitionSpec as P

HD = 128
TILE_TOK = 1601
MAX_TILES = 4
TB = 128
NMAX = 2


neg_fill = -1e30
norm_eps = 1e-05


def passed_along(x, axis, by):
    peers = lax.axis_size(axis)
    pairs = [(i, i + by) for i in range(peers) if 0 <= i + by < peers]
    return lax.ppermute(x, axis, pairs)


def head_major(row_data, kv_local, group_size):
    row_count = row_data.shape[0]
    shaped = row_data.reshape(row_count, kv_local, group_size, HD)
    return shaped.transpose(1, 3, 0, 2).reshape(kv_local, HD, row_count * group_size)


def row_major(head_data, kv_local, group_size):
    row_count = head_data.shape[2] // group_size
    shaped = head_data.reshape(kv_local, HD, row_count, group_size)
    return shaped.transpose(2, 0, 3, 1).reshape(row_count, kv_local * group_size * HD)


def key_product(tile_data, query_cols):
    return lax.dot_general(
        tile_data, query_cols, (((2,), (1,)), ((0,), (0,))), preferred_element_type=jnp.float32
    )


def on_device(
    q_raw,
    out_grad,
    q_gain,
    image_keys,
    image_values,
    block_images,
    image_slot,
    tile_counts,
    q_weight,
):
    heads_local = q_raw.shape[1] // HD
    kv_local = image_keys.shape[2] // HD
    group_size = heads_local // kv_local
    block_width = TB * group_size
    score_scale = 1.0 / math.sqrt(HD)
    images_here = image_keys.shape[0]
    key_count = image_keys.shape[1]
    image_total = image_slot.shape[0]
    block_count = block_images.shape[0]
    raw_rows = q_raw.astype(jnp.float32).reshape(q_raw.shape[0], heads_local, HD)
    inv_rms = lax.rsqrt(jnp.mean(raw_rows * raw_rows, axis=-1, keepdims=True) + norm_eps)
    normed = (raw_rows * inv_rms * q_gain).reshape(q_raw.shape).astype(jnp.bfloat16)
    query_own = head_major(normed, kv_local, group_size)
    cotangent_own = head_major(out_grad, kv_local, group_size)
    own_cols = query_own.shape[2]
    query_next, cotangent_next = passed_along((query_own, cotangent_own), "seq", -1)
    query_all = jnp.concatenate([query_own, query_next], axis=2)
    cotangent_all = jnp.concatenate([cotangent_own, cotangent_next], axis=2)
    column_total = query_all.shape[2]
    device_pos = lax.axis_index("seq")
    slot_ids = device_pos * images_here + jnp.arange(images_here, dtype=jnp.int32)
    matches = image_slot[None, :] == slot_ids[:, None]
    image_ids = jnp.sum(
        jnp.where(matches, jnp.arange(image_total, dtype=jnp.int32)[None, :], 0), axis=1
    )
    tiles_here = jnp.sum(jnp.where(matches, tile_counts[None, :], 0), axis=1)
    first_hits = block_images[:, 0][None, :] == image_ids[:, None]
    first_block = jnp.sum(
        jnp.where(first_hits, jnp.arange(block_count, dtype=jnp.int32)[None, :], 0), axis=1
    )
    readers = 1 + (first_block + 1 < block_count).astype(jnp.int32)
    local_block = first_block - device_pos * images_here
    readers_at = local_block[:, None] + jnp.arange(NMAX, dtype=jnp.int32)[None, :]
    key_heads = image_keys.reshape(images_here, key_count, kv_local, HD).transpose(0, 2, 1, 3)
    value_heads = image_values.reshape(images_here, key_count, kv_local, HD).transpose(0, 2, 1, 3)

    def unit_plan(image_pos):
        unit_total = NMAX * MAX_TILES

        def locate(unit_index):
            pick_index = unit_index // MAX_TILES
            tile_index = unit_index % MAX_TILES
            return (
                pick_index,
                tile_index,
                (pick_index < readers[image_pos]) & (tile_index < tiles_here[image_pos]),
            )

        return (unit_total, locate)

    def unit_data(image_pos, locate, unit_index):
        pick_index, tile_index, is_valid = locate(unit_index)
        block_index = readers_at[image_pos, jnp.minimum(pick_index, NMAX - 1)]
        row_start = block_index * block_width
        key_tile = lax.dynamic_slice_in_dim(
            key_heads[image_pos], tile_index * TILE_TOK, TILE_TOK, 1
        )
        value_tile = lax.dynamic_slice_in_dim(
            value_heads[image_pos], tile_index * TILE_TOK, TILE_TOK, 1
        )
        query_block = lax.dynamic_slice_in_dim(query_all, row_start, block_width, 2)
        cotangent_block = lax.dynamic_slice_in_dim(cotangent_all, row_start, block_width, 2)
        scores = key_product(key_tile, query_block) * score_scale
        return (
            is_valid,
            row_start,
            tile_index,
            key_tile,
            value_tile,
            query_block,
            cotangent_block,
            scores,
        )

    def sweep(unit_step, carry):
        unit_total, locate = unit_plan(0)
        carry = lax.fori_loop(0, unit_total, partial(unit_step, 0, locate), carry)
        return carry

    empty_lse = jnp.full((kv_local, column_total), neg_fill, jnp.float32)
    empty_sum = jnp.zeros((kv_local, column_total), jnp.float32)
    has_left = device_pos > 0

    def norm_step(image_pos, locate, unit_index, lse_rows):
        (
            is_valid,
            row_start,
            tile_index,
            key_tile,
            value_tile,
            query_block,
            cotangent_block,
            scores,
        ) = unit_data(image_pos, locate, unit_index)
        row_top = jnp.max(scores, axis=1)
        tile_lse = row_top + jnp.log(jnp.sum(jnp.exp(scores - row_top[:, None, :]), axis=1))
        previous = lax.dynamic_slice_in_dim(lse_rows, row_start, block_width, 1)
        updated = jnp.where(is_valid, jnp.logaddexp(previous, tile_lse), previous)
        return lax.dynamic_update_slice_in_dim(lse_rows, updated, row_start, 1)

    local_lse = sweep(norm_step, empty_lse)
    came_lse = passed_along(local_lse[:, own_cols:], "seq", 1)
    first_lse = jnp.where(
        has_left, jnp.logaddexp(local_lse[:, :block_width], came_lse), local_lse[:, :block_width]
    )
    own_lse = jnp.concatenate([first_lse, local_lse[:, block_width:own_cols]], axis=1)
    back_lse = passed_along(own_lse, "seq", -1)
    row_lse = jnp.concatenate([own_lse, back_lse], axis=1)

    def delta_step(image_pos, locate, unit_index, delta_rows):
        (
            is_valid,
            row_start,
            tile_index,
            key_tile,
            value_tile,
            query_block,
            cotangent_block,
            scores,
        ) = unit_data(image_pos, locate, unit_index)
        lse_block = lax.dynamic_slice_in_dim(row_lse, row_start, block_width, 1)
        attn_probs = jnp.where(is_valid, jnp.exp(scores - lse_block[:, None, :]), 0.0)
        slopes = key_product(value_tile, cotangent_block)
        previous = lax.dynamic_slice_in_dim(delta_rows, row_start, block_width, 1)
        return lax.dynamic_update_slice_in_dim(
            delta_rows, previous + jnp.sum(attn_probs * slopes, axis=1), row_start, 1
        )

    local_delta = sweep(delta_step, empty_sum)
    came_delta = passed_along(local_delta[:, own_cols:], "seq", 1)
    own_delta = jnp.concatenate(
        [local_delta[:, :block_width] + came_delta, local_delta[:, block_width:own_cols]], axis=1
    )
    back_delta = passed_along(own_delta, "seq", -1)
    row_delta = jnp.concatenate([own_delta, back_delta], axis=1)

    def grad_step(image_pos, locate, unit_index, state):
        rows_grad, key_acc, value_acc = state
        (
            is_valid,
            row_start,
            tile_index,
            key_tile,
            value_tile,
            query_block,
            cotangent_block,
            scores,
        ) = unit_data(image_pos, locate, unit_index)
        lse_block = lax.dynamic_slice_in_dim(row_lse, row_start, block_width, 1)
        delta_block = lax.dynamic_slice_in_dim(row_delta, row_start, block_width, 1)
        attn_probs = jnp.where(is_valid, jnp.exp(scores - lse_block[:, None, :]), 0.0)
        slopes = key_product(value_tile, cotangent_block)
        score_grad = (attn_probs * (slopes - delta_block[:, None, :]) * score_scale).astype(
            jnp.bfloat16
        )
        probs_low = attn_probs.astype(jnp.bfloat16)
        query_part = lax.dot_general(
            key_tile, score_grad, (((1,), (1,)), ((0,), (0,))), preferred_element_type=jnp.float32
        )
        key_part = lax.dot_general(
            score_grad,
            query_block,
            (((2,), (2,)), ((0,), (0,))),
            preferred_element_type=jnp.float32,
        )
        value_part = lax.dot_general(
            probs_low,
            cotangent_block,
            (((2,), (2,)), ((0,), (0,))),
            preferred_element_type=jnp.float32,
        )
        previous = lax.dynamic_slice_in_dim(rows_grad, row_start, block_width, 2)
        rows_grad = lax.dynamic_update_slice_in_dim(rows_grad, previous + query_part, row_start, 2)
        key_start = tile_index * TILE_TOK
        key_old = lax.dynamic_slice_in_dim(key_acc, key_start, TILE_TOK, 1)
        key_acc = lax.dynamic_update_slice_in_dim(key_acc, key_old + key_part, key_start, 1)
        value_old = lax.dynamic_slice_in_dim(value_acc, key_start, TILE_TOK, 1)
        value_acc = lax.dynamic_update_slice_in_dim(value_acc, value_old + value_part, key_start, 1)
        return (rows_grad, key_acc, value_acc)

    rows_grad = jnp.zeros((kv_local, HD, column_total), jnp.float32)
    image_pos = 0
    unit_total, locate = unit_plan(image_pos)
    acc_zero = jnp.zeros((kv_local, key_count, HD), jnp.float32)
    rows_grad, key_acc, value_acc = lax.fori_loop(
        0, unit_total, partial(grad_step, image_pos, locate), (rows_grad, acc_zero, acc_zero)
    )
    key_grads = [key_acc]
    value_grads = [value_acc]
    key_grad = (
        jnp.stack(key_grads).transpose(0, 2, 1, 3).reshape(image_keys.shape).astype(jnp.bfloat16)
    )
    value_grad = (
        jnp.stack(value_grads)
        .transpose(0, 2, 1, 3)
        .reshape(image_values.shape)
        .astype(jnp.bfloat16)
    )
    came_grad = passed_along(rows_grad[:, :, own_cols:].astype(jnp.bfloat16), "seq", 1).astype(
        jnp.float32
    )
    own_grad = jnp.concatenate(
        [rows_grad[:, :, :block_width] + came_grad, rows_grad[:, :, block_width:own_cols]], axis=2
    )
    normed_grad = row_major(own_grad, kv_local, group_size).reshape(q_raw.shape[0], heads_local, HD)
    scaled = normed_grad * q_gain
    raw_grad = inv_rms * scaled - raw_rows * (inv_rms * inv_rms * inv_rms) * jnp.mean(
        scaled * raw_rows, axis=-1, keepdims=True
    )
    raw_grad = raw_grad.reshape(q_raw.shape).astype(jnp.bfloat16)
    text_grad = lax.psum_scatter(
        lax.dot_general(
            raw_grad, q_weight, (((1,), (1,)), ((), ())), preferred_element_type=jnp.float32
        ).astype(jnp.bfloat16),
        "tp",
        scatter_dimension=0,
        tiled=True,
    )
    return (text_grad, key_grad, value_grad)


def solution(mesh):
    return jax.shard_map(
        on_device,
        mesh=mesh,
        in_specs=(
            P("seq", "tp"),
            P("seq", "tp"),
            P(),
            P("seq", None, "tp"),
            P("seq", None, "tp"),
            P(),
            P(),
            P(),
            P(None, "tp"),
        ),
        out_specs=(P(("seq", "tp"), None), P("seq", None, "tp"), P("seq", None, "tp")),
        check_vma=False,
    )
```

profile of v0, /device:TPU:0, one launch (start us, length us, event | category | flops | bytes accessed | tf_op | source)
XLA Modules:
  0.0 590.1 jit_solution(10262264317952841826)
XLA Ops:
  24.2 50.9 %while.49 = (s32[]{:T(128)}, f32[1,2048]{1,0:T(1,128)S(1)}, s32[1]{0:T(128)}, s32[1]{0:T(128)}, s32[1,2]{1,0:T(1,128)S(1)}, /*index=5*/bf16[1,6404,128]{2,1,0:T(...) while((s32[]{:T(128)}, f32[1,2048]{1,0:T(1,128)S(1)}, ...), condition=%wide.region_7.8_spmd, body=%wide.region_4.7_spmd.sunk | while | flops 427897888 | bytes 13826492 | solution.py:131
  75.1 3.9 collective-permute-start.1
  82.7 3.4 collective-permute-done.2
  86.8 107.7 %while.50 = (s32[]{:T(128)}, f32[1,2048]{1,0:T(1,128)S(1)}, s32[1,2]{1,0:T(1,128)S(1)}, s32[1]{0:T(128)}, s32[1]{0:T(128)}, /*index=5*/bf16[1,6404,128]{2,1,0:T(...) while((s32[]{:T(128)}, f32[1,2048]{1,0:T(1,128)S(1)}, ...), condition=%wide.region_10.11_spmd, body=%wide.region_8.10_spmd.sunk | while | flops 847582208 | bytes 14520800 | solution.py:131
  89.3 4.8 fusion.102
  95.3 4.8 multiply_reduce_fusion.6
  102.8 4.8 fusion.102
  108.8 4.8 multiply_reduce_fusion.6
  116.2 4.8 fusion.102
  122.3 4.8 multiply_reduce_fusion.6
  129.7 4.8 fusion.102
  135.7 4.8 multiply_reduce_fusion.6
  143.2 4.8 fusion.102
  149.2 4.8 multiply_reduce_fusion.6
  156.6 4.8 fusion.102
  162.7 4.8 multiply_reduce_fusion.6
  170.1 4.8 fusion.102
  176.1 4.8 multiply_reduce_fusion.6
  183.6 4.8 fusion.102
  189.6 4.8 multiply_reduce_fusion.6
  194.5 5.3 collective-permute-start.4
  202.6 4.3 collective-permute-done.5
  212.4 302.6 %while.51 = (s32[]{:T(128)}, f32[1,128,2048]{1,2,0:T(8,128)}, f32[1,6404,128]{2,1,0:T(8,128)}, f32[1,6404,128]{2,1,0:T(8,128)}, s32[1,2]{1,0:T(1,128)S(1)}, /*in...) while((s32[]{:T(128)}, f32[1,128,2048]{1,2,0:T(8,128)}, ...), condition=%wide.region_12.13_spmd, body=%wide.region_11.12_spmd.sunk | while | flops 2117037312 | bytes 49979108 | solution.py:239
  217.0 4.8 fusion.114
  223.6 5.2 multiply_convert_fusion.2
  238.5 3.7 dynamic_update_slice.61
  242.2 4.5 fusion.117
  246.7 3.5 dynamic_update_slice.62
  254.9 4.8 fusion.114
  261.6 5.2 multiply_convert_fusion.2
  276.4 3.7 dynamic_update_slice.61
  280.1 4.5 fusion.117
  284.7 3.5 dynamic_update_slice.62
  292.9 4.8 fusion.114
  299.6 5.2 multiply_convert_fusion.2
  314.4 3.8 dynamic_update_slice.61
  318.2 4.5 fusion.117
  322.7 3.5 dynamic_update_slice.62
  330.9 4.8 fusion.114
  337.6 5.2 multiply_convert_fusion.2
  352.4 3.4 dynamic_update_slice.61
  355.9 4.5 fusion.117
  368.3 4.8 fusion.114
  375.0 5.2 multiply_convert_fusion.2
  389.8 3.7 dynamic_update_slice.61
  393.5 4.5 fusion.117
  398.1 3.5 dynamic_update_slice.62
  406.3 4.8 fusion.114
  412.9 5.2 multiply_convert_fusion.2
  427.8 3.7 dynamic_update_slice.61
  431.5 4.5 fusion.117
  436.0 3.5 dynamic_update_slice.62
  444.2 4.8 fusion.114
  450.9 5.2 multiply_convert_fusion.2
  465.8 3.8 dynamic_update_slice.61
  469.5 4.5 fusion.117
  474.1 3.5 dynamic_update_slice.62
  482.3 4.8 fusion.114
  488.9 5.2 multiply_convert_fusion.2
  503.8 3.4 dynamic_update_slice.61
  507.2 4.5 fusion.117
  516.0 6.3 %collective-permute-start.6 = (bf16[1,128,1024]{1,2,0:T(8,128)(2,1)S(1)}, bf16[1,128,1024]{1,2,0:T(8,128)(2,1)S(1)}, u32[]{:S(2)}, u32[]{:S(2)}) collective-permute-start(bf16[1,128,1024]{1,2,0:T(8,128)(2,1)S(1)} %slice.36), channel_id=1, source_target_pairs={{0,8},{8,16},{16,24},{24,32},{32,40},{40,48},{48,56},{56,64},{64,7... | collective-permute-start | bytes 786440 | tf_op jit(solution)/shard_map/ppermute | solution.py:23
  530.2 13.6 %convolution_convert_fusion = bf16[128,8192]{1,0:T(8,128)(2,1)} fusion(bf16[8192,1024]{1,0:T(8,128)(2,1)} %param.23, bf16[128,1024]{1,0:T(8,128)(2,1)S(1)} %copy-done.7, f32[16,8,8,128]{3,2,1,0:T(8,128)} %bitcast.200, f32[16,8,8,128]{3,2,1,0:T(8,128)} %bitcast.201, f32[16,8,8,128]{3,2,1,0:T(8,128)} %bitcast.202, f32[16,8,8,128]{3,2,1,0:T(8,128)} %bitcast.197, ...), kind=kOutput, calls=%fused_computation.66 | convolution fusion | flops 2149449728 | bytes 21237760 | tf_op jit(solution)/shard_map/dot_general | solution.py:266
  547.6 35.6 %reduce-scatter.2.cloned.1.call-done = bf16[16,8192]{1,0:T(8,128)(2,1)} async-done(((bf16[128,8192]{1,0:T(8,128)(2,1)}), bf16[16,8192]{1,0:T(8,128)(2,1)}) %reduce-scatter.2.cloned.1.call-update) | async-done | bytes 262160 | tf_op jit(solution)/shard_map/reduce_scatter | solution.py:265
  (272 shorter events, 197.5 us)
Async XLA Ops:
  7.2 576.1 %reduce-scatter.2.cloned.1.call-start = ((), (), s32[]{:S(2)}) async-start(), calls=%async_computation.1 | async-start | bytes 2359296 | tf_op jit(solution)/shard_map/reduce_scatter | solution.py:265
  8.3 0.8 copy-start.6
  10.7 4.5 copy-start.8
  10.9 0.8 copy-start.5
  12.9 11.1 %collective-permute-start = (bf16[1,128,1024]{1,2,0:T(8,128)(2,1)S(1)}, bf16[1,128,1024]{1,2,0:T(8,128)(2,1)S(1)}, u32[]{:S(2)}, u32[]{:S(2)}) collective-permute-start(bf16[1,128,1024]{1,2,0:T(8,128)(2,1)S(1)} %bitcast.205), channel_id=1, source_target_pairs={{8,0},{16,8},{24,16},{32,24},{40,32},{48,40},{56,48},{64,56},{72,6... | collective-permute-start | bytes 786440 | tf_op jit(solution)/shard_map/ppermute | solution.py:23
  15.2 66.5 %collective-permute-start.3 = (bf16[1,128,1024]{1,2,0:T(8,128)(2,1)S(1)}, bf16[1,128,1024]{1,2,0:T(8,128)(2,1)S(1)}, u32[]{:S(2)}, u32[]{:S(2)}) collective-permute-start(bf16[1,128,1024]{1,2,0:T(8,128)(2,1)S(1)} %bitcast.203), channel_id=1, source_target_pairs={{8,0},{16,8},{24,16},{32,24},{40,32},{48,40},{56,48},{64,56},{72,6... | collective-permute-start | bytes 786440 | tf_op jit(solution)/shard_map/ppermute | solution.py:23
  75.1 5.2 collective-permute-start.1
  80.4 5.8 collective-permute-start.2
  194.5 6.6 %collective-permute-start.4 = (f32[1,1024]{1,0:T(1,128)S(1)}, f32[1,1024]{1,0:T(1,128)S(1)}, u32[]{:S(2)}, u32[]{:S(2)}) collective-permute-start(f32[1,1024]{1,0:T(1,128)S(1)} %slice.27), channel_id=1, source_target_pairs={{0,8},{8,16},{16,24},{24,32},{32,40},{40,48},{48,56},{56,64},{64,7... | collective-permute-start | bytes 12296 | tf_op jit(solution)/shard_map/ppermute | solution.py:23
  201.1 5.8 collective-permute-start.5
  212.4 317.8 %copy-start.7 = (bf16[128,1024]{1,0:T(8,128)(2,1)S(1)}, bf16[128,1024]{1,0:T(8,128)(2,1)}, u32[]{:S(2)}) copy-start(bf16[128,1024]{1,0:T(8,128)(2,1)} %param.15) | copy-start | bytes 786436
  212.4 9.4 %copy-start = (bf16[1,128,2048]{2,1,0:T(8,128)(2,1)}, bf16[1,128,2048]{2,1,0:T(8,128)(2,1)S(1)}, u32[]{:S(2)}) copy-start(bf16[1,128,2048]{2,1,0:T(8,128)(2,1)S(1)} %get-tuple-element.1253) | copy-start | bytes 1572868 | tf_op jit(solution)/shard_map/while
  212.4 9.4 %copy-start.9 = (s32[1,2]{1,0:T(1,128)}, s32[1,2]{1,0:T(1,128)S(1)}, u32[]{:S(2)}) copy-start(s32[1,2]{1,0:T(1,128)S(1)} %get-tuple-element.1249) | copy-start | bytes 28 | tf_op jit(solution)/shard_map/while
  223.6 5.2 copy-start.2
  238.5 11.7 %copy-start.1 = (bf16[1,128,2048]{2,1,0:T(8,128)(2,1)S(1)}, bf16[1,128,2048]{2,1,0:T(8,128)(2,1)}, u32[]{:S(2)}) copy-start(bf16[1,128,2048]{2,1,0:T(8,128)(2,1)} %copy-done) | copy-start | bytes 1572868 | tf_op jit(solution)/shard_map/while
  238.5 11.7 %copy-start.10 = (s32[1,2]{1,0:T(1,128)S(1)}, s32[1,2]{1,0:T(1,128)}, u32[]{:S(2)}) copy-start(s32[1,2]{1,0:T(1,128)} %copy-done.9) | copy-start | bytes 28 | tf_op jit(solution)/shard_map/while
  250.2 9.5 %copy-start = (bf16[1,128,2048]{2,1,0:T(8,128)(2,1)}, bf16[1,128,2048]{2,1,0:T(8,128)(2,1)S(1)}, u32[]{:S(2)}) copy-start(bf16[1,128,2048]{2,1,0:T(8,128)(2,1)S(1)} %get-tuple-element.1253) | copy-start | bytes 1572868 | tf_op jit(solution)/shard_map/while
  250.2 9.5 %copy-start.9 = (s32[1,2]{1,0:T(1,128)}, s32[1,2]{1,0:T(1,128)S(1)}, u32[]{:S(2)}) copy-start(s32[1,2]{1,0:T(1,128)S(1)} %get-tuple-element.1249) | copy-start | bytes 28 | tf_op jit(solution)/shard_map/while
  261.6 5.2 copy-start.2
  276.4 11.8 %copy-start.1 = (bf16[1,128,2048]{2,1,0:T(8,128)(2,1)S(1)}, bf16[1,128,2048]{2,1,0:T(8,128)(2,1)}, u32[]{:S(2)}) copy-start(bf16[1,128,2048]{2,1,0:T(8,128)(2,1)} %copy-done) | copy-start | bytes 1572868 | tf_op jit(solution)/shard_map/while
  276.4 11.8 %copy-start.10 = (s32[1,2]{1,0:T(1,128)S(1)}, s32[1,2]{1,0:T(1,128)}, u32[]{:S(2)}) copy-start(s32[1,2]{1,0:T(1,128)} %copy-done.9) | copy-start | bytes 28 | tf_op jit(solution)/shard_map/while
  288.2 9.5 %copy-start = (bf16[1,128,2048]{2,1,0:T(8,128)(2,1)}, bf16[1,128,2048]{2,1,0:T(8,128)(2,1)S(1)}, u32[]{:S(2)}) copy-start(bf16[1,128,2048]{2,1,0:T(8,128)(2,1)S(1)} %get-tuple-element.1253) | copy-start | bytes 1572868 | tf_op jit(solution)/shard_map/while
  288.2 9.5 %copy-start.9 = (s32[1,2]{1,0:T(1,128)}, s32[1,2]{1,0:T(1,128)S(1)}, u32[]{:S(2)}) copy-start(s32[1,2]{1,0:T(1,128)S(1)} %get-tuple-element.1249) | copy-start | bytes 28 | tf_op jit(solution)/shard_map/while
  299.6 5.2 copy-start.2
  314.4 11.8 %copy-start.1 = (bf16[1,128,2048]{2,1,0:T(8,128)(2,1)S(1)}, bf16[1,128,2048]{2,1,0:T(8,128)(2,1)}, u32[]{:S(2)}) copy-start(bf16[1,128,2048]{2,1,0:T(8,128)(2,1)} %copy-done) | copy-start | bytes 1572868 | tf_op jit(solution)/shard_map/while
  314.4 11.8 %copy-start.10 = (s32[1,2]{1,0:T(1,128)S(1)}, s32[1,2]{1,0:T(1,128)}, u32[]{:S(2)}) copy-start(s32[1,2]{1,0:T(1,128)} %copy-done.9) | copy-start | bytes 28 | tf_op jit(solution)/shard_map/while
  326.2 9.5 %copy-start = (bf16[1,128,2048]{2,1,0:T(8,128)(2,1)}, bf16[1,128,2048]{2,1,0:T(8,128)(2,1)S(1)}, u32[]{:S(2)}) copy-start(bf16[1,128,2048]{2,1,0:T(8,128)(2,1)S(1)} %get-tuple-element.1253) | copy-start | bytes 1572868 | tf_op jit(solution)/shard_map/while
  326.2 9.5 %copy-start.9 = (s32[1,2]{1,0:T(1,128)}, s32[1,2]{1,0:T(1,128)S(1)}, u32[]{:S(2)}) copy-start(s32[1,2]{1,0:T(1,128)S(1)} %get-tuple-element.1249) | copy-start | bytes 28 | tf_op jit(solution)/shard_map/while
  337.6 5.2 copy-start.2
  352.4 11.2 %copy-start.1 = (bf16[1,128,2048]{2,1,0:T(8,128)(2,1)S(1)}, bf16[1,128,2048]{2,1,0:T(8,128)(2,1)}, u32[]{:S(2)}) copy-start(bf16[1,128,2048]{2,1,0:T(8,128)(2,1)} %copy-done) | copy-start | bytes 1572868 | tf_op jit(solution)/shard_map/while
  352.4 11.2 %copy-start.10 = (s32[1,2]{1,0:T(1,128)S(1)}, s32[1,2]{1,0:T(1,128)}, u32[]{:S(2)}) copy-start(s32[1,2]{1,0:T(1,128)} %copy-done.9) | copy-start | bytes 28 | tf_op jit(solution)/shard_map/while
  363.6 9.5 %copy-start = (bf16[1,128,2048]{2,1,0:T(8,128)(2,1)}, bf16[1,128,2048]{2,1,0:T(8,128)(2,1)S(1)}, u32[]{:S(2)}) copy-start(bf16[1,128,2048]{2,1,0:T(8,128)(2,1)S(1)} %get-tuple-element.1253) | copy-start | bytes 1572868 | tf_op jit(solution)/shard_map/while
  363.6 9.5 %copy-start.9 = (s32[1,2]{1,0:T(1,128)}, s32[1,2]{1,0:T(1,128)S(1)}, u32[]{:S(2)}) copy-start(s32[1,2]{1,0:T(1,128)S(1)} %get-tuple-element.1249) | copy-start | bytes 28 | tf_op jit(solution)/shard_map/while
  375.0 5.2 copy-start.2
  389.8 11.7 %copy-start.1 = (bf16[1,128,2048]{2,1,0:T(8,128)(2,1)S(1)}, bf16[1,128,2048]{2,1,0:T(8,128)(2,1)}, u32[]{:S(2)}) copy-start(bf16[1,128,2048]{2,1,0:T(8,128)(2,1)} %copy-done) | copy-start | bytes 1572868 | tf_op jit(solution)/shard_map/while
  389.8 11.7 %copy-start.10 = (s32[1,2]{1,0:T(1,128)S(1)}, s32[1,2]{1,0:T(1,128)}, u32[]{:S(2)}) copy-start(s32[1,2]{1,0:T(1,128)} %copy-done.9) | copy-start | bytes 28 | tf_op jit(solution)/shard_map/while
  401.6 9.5 %copy-start = (bf16[1,128,2048]{2,1,0:T(8,128)(2,1)}, bf16[1,128,2048]{2,1,0:T(8,128)(2,1)S(1)}, u32[]{:S(2)}) copy-start(bf16[1,128,2048]{2,1,0:T(8,128)(2,1)S(1)} %get-tuple-element.1253) | copy-start | bytes 1572868 | tf_op jit(solution)/shard_map/while
  401.6 9.5 %copy-start.9 = (s32[1,2]{1,0:T(1,128)}, s32[1,2]{1,0:T(1,128)S(1)}, u32[]{:S(2)}) copy-start(s32[1,2]{1,0:T(1,128)S(1)} %get-tuple-element.1249) | copy-start | bytes 28 | tf_op jit(solution)/shard_map/while
  412.9 5.2 copy-start.2
  427.8 11.8 %copy-start.1 = (bf16[1,128,2048]{2,1,0:T(8,128)(2,1)S(1)}, bf16[1,128,2048]{2,1,0:T(8,128)(2,1)}, u32[]{:S(2)}) copy-start(bf16[1,128,2048]{2,1,0:T(8,128)(2,1)} %copy-done) | copy-start | bytes 1572868 | tf_op jit(solution)/shard_map/while
  427.8 11.8 %copy-start.10 = (s32[1,2]{1,0:T(1,128)S(1)}, s32[1,2]{1,0:T(1,128)}, u32[]{:S(2)}) copy-start(s32[1,2]{1,0:T(1,128)} %copy-done.9) | copy-start | bytes 28 | tf_op jit(solution)/shard_map/while
  439.5 9.5 %copy-start = (bf16[1,128,2048]{2,1,0:T(8,128)(2,1)}, bf16[1,128,2048]{2,1,0:T(8,128)(2,1)S(1)}, u32[]{:S(2)}) copy-start(bf16[1,128,2048]{2,1,0:T(8,128)(2,1)S(1)} %get-tuple-element.1253) | copy-start | bytes 1572868 | tf_op jit(solution)/shard_map/while
  439.5 9.5 %copy-start.9 = (s32[1,2]{1,0:T(1,128)}, s32[1,2]{1,0:T(1,128)S(1)}, u32[]{:S(2)}) copy-start(s32[1,2]{1,0:T(1,128)S(1)} %get-tuple-element.1249) | copy-start | bytes 28 | tf_op jit(solution)/shard_map/while
  450.9 5.2 copy-start.2
  465.8 11.8 %copy-start.1 = (bf16[1,128,2048]{2,1,0:T(8,128)(2,1)S(1)}, bf16[1,128,2048]{2,1,0:T(8,128)(2,1)}, u32[]{:S(2)}) copy-start(bf16[1,128,2048]{2,1,0:T(8,128)(2,1)} %copy-done) | copy-start | bytes 1572868 | tf_op jit(solution)/shard_map/while
  465.8 11.8 %copy-start.10 = (s32[1,2]{1,0:T(1,128)S(1)}, s32[1,2]{1,0:T(1,128)}, u32[]{:S(2)}) copy-start(s32[1,2]{1,0:T(1,128)} %copy-done.9) | copy-start | bytes 28 | tf_op jit(solution)/shard_map/while
  477.5 9.5 %copy-start = (bf16[1,128,2048]{2,1,0:T(8,128)(2,1)}, bf16[1,128,2048]{2,1,0:T(8,128)(2,1)S(1)}, u32[]{:S(2)}) copy-start(bf16[1,128,2048]{2,1,0:T(8,128)(2,1)S(1)} %get-tuple-element.1253) | copy-start | bytes 1572868 | tf_op jit(solution)/shard_map/while
  477.6 9.5 %copy-start.9 = (s32[1,2]{1,0:T(1,128)}, s32[1,2]{1,0:T(1,128)S(1)}, u32[]{:S(2)}) copy-start(s32[1,2]{1,0:T(1,128)S(1)} %get-tuple-element.1249) | copy-start | bytes 28 | tf_op jit(solution)/shard_map/while
  488.9 5.2 copy-start.2
  503.7 11.2 %copy-start.1 = (bf16[1,128,2048]{2,1,0:T(8,128)(2,1)S(1)}, bf16[1,128,2048]{2,1,0:T(8,128)(2,1)}, u32[]{:S(2)}) copy-start(bf16[1,128,2048]{2,1,0:T(8,128)(2,1)} %copy-done) | copy-start | bytes 1572868 | tf_op jit(solution)/shard_map/while
  503.8 11.2 %copy-start.10 = (s32[1,2]{1,0:T(1,128)S(1)}, s32[1,2]{1,0:T(1,128)}, u32[]{:S(2)}) copy-start(s32[1,2]{1,0:T(1,128)} %copy-done.9) | copy-start | bytes 28 | tf_op jit(solution)/shard_map/while
  516.0 9.9 %collective-permute-start.6 = (bf16[1,128,1024]{1,2,0:T(8,128)(2,1)S(1)}, bf16[1,128,1024]{1,2,0:T(8,128)(2,1)S(1)}, u32[]{:S(2)}, u32[]{:S(2)}) collective-permute-start(bf16[1,128,1024]{1,2,0:T(8,128)(2,1)S(1)} %slice.36), channel_id=1, source_target_pairs={{0,8},{8,16},{16,24},{24,32},{32,40},{40,48},{48,56},{56,64},{64,7... | collective-permute-start | bytes 786440 | tf_op jit(solution)/shard_map/ppermute | solution.py:23
  530.2 13.6 %copy-start.3 = (f32[1,6404,128]{2,1,0:T(8,128)S(1)}, f32[1,6404,128]{2,1,0:T(8,128)}, u32[]{:S(2)}) copy-start(f32[1,6404,128]{2,1,0:T(8,128)} %get-tuple-element.743) | copy-start | bytes 9836548
  543.8 2.5 copy-start.4
Sparse Core Ops, SparseCore 0:
  543.9 39.3 reduce-scatter.1
where the time goes:
time: 596 us; the launch traced here: 590 us
  matrix products  268 us (45%)
  local copies, waits for them, and re-layouts  136 us (23%)
  loops' own time  61.7 us (10%)
  waiting for transfers between devices  51.7 us (9%)
  other arithmetic  36.4 us (6%)
  starting transfers between devices  20.9 us (4%)
  between operations  15.6 us (3%)
    dot_general x40, matrix products, key_product(): lax.dot_general(tile_data, query_cols, (((2,), (1,)), ((0,), (0,))), pref...  173 us
    another operation x2, loops' own time, sweep(): carry = lax.fori_loop(0, unit_total, partial(unit_step, 0, locate), carry)  41 us
    dot_general x8, matrix products, grad_step(): lax.dot_general(probs_low, cotangent_block, (((2,), (2,)), ((0,), (0,))),...  36.3 us
    reduce_scatter x1, waiting for transfers between devices, on_device(): lax.psum_scatter(lax.dot_general(raw_grad, q_weight, (((1,), (1,)), ((),...  35.6 us
    dynamic_update_slice x16, local copies, waits for them, and re-layouts, grad_step(): lax.dynamic_update_slice_in_dim(rows_grad, previous + query_part, row_sta...  31.4 us
    dynamic_update_slice x8, local copies, waits for them, and re-layouts, grad_step(): lax.dynamic_update_slice_in_dim(key_acc, key_old + key_part, key_start, 1)  29.2 us
    dynamic_update_slice x8, local copies, waits for them, and re-layouts, grad_step(): lax.dynamic_update_slice_in_dim(value_acc, value_old + value_part, key_st...  27.4 us
    dot_general x8, matrix products, grad_step(): lax.dot_general(score_grad, query_block, (((2,), (2,)), ((0,), (0,))), pr...  25.3 us
  transfers between devices with their start and end apart: 8, of which 7 were waited for; matrix products, arithmetic and copies ran while one was open for 7% of the time, Pallas kernels for 0%

commit v1 on v0

v1 whole, which is shorter than its diff:
```python
import functools
import math

import jax
import jax.numpy as jnp
from jax import lax
from jax.experimental import pallas as pl
from jax.experimental.pallas import tpu as pltpu
from jax.sharding import PartitionSpec as P

HD = 128
TILE_TOK = 1601
CHUNK = 512
GROUP = 256
norm_eps = 1e-05
score_scale = 1.0 / math.sqrt(HD)
exp2_scale = score_scale * math.log2(math.e)
MESH = pl.DeviceIdType.MESH
bf16, f32 = jnp.bfloat16, jnp.float32


def nn(a, b):
    return jnp.dot(a, b, preferred_element_type=f32)


def nt(a, b):
    return lax.dot_general(a, b, (((1,), (1,)), ((), ())), preferred_element_type=f32)


def attention_kernel(
    limit_ref,
    q_ref,
    g_ref,
    gain_ref,
    key_ref,
    value_ref,
    raw_out,
    key_out,
    value_out,
    keys,
    values,
    keys_t,
    values_t,
    qt,
    gt,
    e_all,
    m_all,
    acc,
    dkt,
    dvt,
    dqt,
    stats_own,
    stats_send,
    stats_in,
    total,
    total_in,
    dq_send,
    dq_in,
    send_sem,
    recv_sem,
):
    seq = lax.axis_index("seq")
    tp = lax.axis_index("tp")
    seq_size = lax.axis_size("seq")
    has_left = seq > 0
    has_next = seq < seq_size - 1
    left = (jnp.maximum(seq - 1, 0), tp)
    right = (jnp.minimum(seq + 1, seq_size - 1), tp)
    heads = q_ref.shape[1] // HD
    cols = q_ref.shape[1]
    key_count = key_ref.shape[1]
    padded = keys.shape[0]
    chunks = padded // CHUNK
    groups = cols // GROUP
    limit = limit_ref[0]

    barrier = pltpu.get_barrier_semaphore()

    for step in (1, seq_size - 1):
        near = (lax.rem(seq + step, seq_size), tp)
        pl.semaphore_signal(barrier, inc=1, device_id=near, device_id_type=MESH)

    def rdma(index, src, dst, device):
        return pltpu.make_async_remote_copy(
            src_ref=src,
            dst_ref=dst,
            send_sem=send_sem.at[index],
            recv_sem=recv_sem.at[index],
            device_id=device,
            device_id_type=MESH,
        )

    q_copy = rdma(0, qt.at[0], qt.at[1], left)
    g_copy = rdma(1, gt.at[0], gt.at[1], left)
    stats_copy = rdma(2, stats_send, stats_in, right)
    total_copy = rdma(3, total.at[0], total_in, left)
    dq_copy = rdma(4, dq_send, dq_in, right)

    gain = gain_ref[...]
    for h in range(heads):
        span = slice(h * HD, (h + 1) * HD)
        raw = q_ref[:, span].astype(f32)
        inv = lax.rsqrt(jnp.mean(raw * raw, axis=-1, keepdims=True) + norm_eps)
        normed = raw * inv * gain
        qt[0, :, span] = normed.T.astype(bf16)
        gt[0, :, span] = g_ref[:, span].T

    pl.semaphore_wait(barrier, 2)

    @pl.when(has_left)
    def _():
        q_copy.start()
        g_copy.start()

    first_key = key_ref[0, 0:1, :]

    def fill(start, rows, key_rows, value_rows):
        held = key_rows.shape[0]
        at = start + lax.broadcasted_iota(jnp.int32, (rows, HD), 0)
        if held < rows:
            pad = jnp.zeros((rows - held, HD), bf16)
            key_rows = jnp.concatenate([key_rows, pad], axis=0)
            value_rows = jnp.concatenate([value_rows, pad], axis=0)
        live = at < limit
        key_f = key_rows.astype(f32)
        value_low = jnp.where(live, value_rows.astype(f32), 0.0).astype(bf16)
        keys[pl.ds(start, rows), :] = jnp.where(live, key_f, first_key.astype(f32)).astype(bf16)
        values[pl.ds(start, rows), :] = value_low
        keys_t[:, pl.ds(start, rows)] = jnp.where(live, key_f, 0.0).astype(bf16).T
        values_t[0:HD, pl.ds(start, rows)] = value_low.T
        live_t = start + lax.broadcasted_iota(jnp.int32, (16, rows), 1) < limit
        values_t[HD : HD + 16, pl.ds(start, rows)] = jnp.where(live_t, 1.0, 0.0).astype(bf16)

    def fill_step(i, carry):
        start = pl.multiple_of(i * CHUNK, CHUNK)
        fill(start, CHUNK, key_ref[0, pl.ds(start, CHUNK), :], value_ref[0, pl.ds(start, CHUNK), :])
        return carry

    whole = key_count // CHUNK
    lax.fori_loop(0, whole, fill_step, 0)
    if whole < chunks:
        tail = whole * CHUNK
        fill(tail, CHUNK, key_ref[0, tail:key_count, :], value_ref[0, tail:key_count, :])

    def totals_pass(b, stats):
        acc[...] = jnp.zeros_like(acc)
        stats[0:1, :] = jnp.full((1, cols), -1e30, f32)

        def step(i, carry):
            start = pl.multiple_of(i * CHUNK, CHUNK)
            key_chunk = keys[pl.ds(start, CHUNK), :]
            value_chunk = values_t[:, pl.ds(start, CHUNK)]

            def product(j):
                return nn(key_chunk, qt[b, :, j * GROUP : (j + 1) * GROUP])

            scores = product(0)
            for j in range(groups):
                later = product(j + 1) if j + 1 < groups else None
                span = slice(j * GROUP, (j + 1) * GROUP)
                before = stats[0:1, span]
                top = jnp.maximum(before, jnp.max(scores, axis=0, keepdims=True) * exp2_scale)
                stats[0:1, span] = top
                m_all[b, i, 0:1, span] = top
                low = jnp.exp2(scores * exp2_scale - top).astype(bf16)
                e_all[b, pl.ds(start, CHUNK), span] = low
                acc[:, span] = acc[:, span] * jnp.exp2(before - top) + nn(value_chunk, low)
                scores = later
            return carry

        lax.fori_loop(0, chunks, step, 0)
        stats[1:2, :] = acc[HD : HD + 1, :]

    def finish_totals(b, stats):
        stats[2:3, :] = jnp.sum(acc[0:HD, :] * gt[b].astype(f32), axis=0, keepdims=True)

    totals_pass(0, stats_own)
    finish_totals(0, stats_own)

    @pl.when(has_next)
    def _():
        q_copy.wait_recv()
        totals_pass(1, stats_send)
        g_copy.wait_recv()
        finish_totals(1, stats_send)
        stats_copy.start()

    @pl.when(has_left)
    def _():
        stats_copy.wait_recv()
        m1, l1, d1 = stats_own[0:1, :], stats_own[1:2, :], stats_own[2:3, :]
        m2, l2, d2 = stats_in[0:1, :], stats_in[1:2, :], stats_in[2:3, :]
        top = jnp.maximum(m1, m2)
        w1, w2 = jnp.exp2(m1 - top), jnp.exp2(m2 - top)
        norm = l1 * w1 + l2 * w2
        total[0, 0:1, :] = top + jnp.log2(norm)
        total[0, 1:2, :] = (d1 * w1 + d2 * w2) / norm
        total_copy.start()

    @pl.when(jnp.logical_not(has_left))
    def _():
        norm = stats_own[1:2, :]
        total[0, 0:1, :] = stats_own[0:1, :] + jnp.log2(norm)
        total[0, 1:2, :] = stats_own[2:3, :] / norm

    def grads_pass(b, totals, write):
        dqt[...] = jnp.zeros_like(dqt)

        def step(i, carry):
            start = pl.multiple_of(i * CHUNK, CHUNK)
            value_chunk = values[pl.ds(start, CHUNK), :]
            key_chunk = keys_t[:, pl.ds(start, CHUNK)]

            def product(j):
                return nn(value_chunk, gt[b, :, j * GROUP : (j + 1) * GROUP])

            slopes = product(0)
            key_part, value_part = None, None
            for j in range(groups):
                later = product(j + 1) if j + 1 < groups else None
                span = slice(j * GROUP, (j + 1) * GROUP)
                weight = jnp.exp2(m_all[b, i, 0:1, span] - totals[0:1, span])
                probs = e_all[b, pl.ds(start, CHUNK), span].astype(f32) * weight
                probs_low = probs.astype(bf16)
                score_grad = (probs * (slopes - totals[1:2, span])).astype(bf16)
                v_part = nt(gt[b, :, span], probs_low)
                k_part = nt(qt[b, :, span], score_grad)
                dqt[:, span] += nn(key_chunk, score_grad)
                key_part = k_part if j == 0 else key_part + k_part
                value_part = v_part if j == 0 else value_part + v_part
                slopes = later
            write(start, key_part, value_part)
            return carry

        lax.fori_loop(0, chunks, step, 0)

    def hold(start, key_part, value_part):
        dkt[:, pl.ds(start, CHUNK)] = key_part
        dvt[:, pl.ds(start, CHUNK)] = value_part

    def emit(start, key_part, value_part):
        hold(start, key_part + dkt[:, pl.ds(start, CHUNK)], value_part + dvt[:, pl.ds(start, CHUNK)])

    @pl.when(has_next)
    def _():
        total_copy.wait_recv()
        grads_pass(1, total_in, hold)
        dq_send[...] = dqt[...].astype(bf16)
        dq_copy.start()

    @pl.when(jnp.logical_not(has_next))
    def _():
        dkt[...] = jnp.zeros_like(dkt)
        dvt[...] = jnp.zeros_like(dvt)

    grads_pass(0, total.at[0], emit)

    def output(start, rows):
        live = start + lax.broadcasted_iota(jnp.int32, (rows, HD), 0) < limit
        span = pl.ds(start, CHUNK)
        key_rows = (dkt[:, span] * score_scale).T[0:rows]
        value_rows = dvt[:, span].T[0:rows]
        key_out[0, pl.ds(start, rows), :] = jnp.where(live, key_rows, 0.0).astype(bf16)
        value_out[0, pl.ds(start, rows), :] = jnp.where(live, value_rows, 0.0).astype(bf16)

    def output_step(i, carry):
        output(pl.multiple_of(i * CHUNK, CHUNK), CHUNK)
        return carry

    lax.fori_loop(0, whole, output_step, 0)
    if whole < chunks:
        output(whole * CHUNK, key_count - whole * CHUNK)

    @pl.when(has_left)
    def _():
        dq_copy.wait_recv()
        dqt[...] += dq_in[...].astype(f32)

    for h in range(heads):
        span = slice(h * HD, (h + 1) * HD)
        raw = q_ref[:, span].astype(f32)
        inv = lax.rsqrt(jnp.mean(raw * raw, axis=-1, keepdims=True) + norm_eps)
        scaled = dqt[:, span].T * score_scale * gain
        spread = jnp.mean(scaled * raw, axis=-1, keepdims=True)
        raw_out[:, span] = (inv * scaled - raw * (inv * inv * inv) * spread).astype(bf16)

    @pl.when(has_left)
    def _():
        q_copy.wait_send()
        g_copy.wait_send()
        total_copy.wait_send()

    @pl.when(has_next)
    def _():
        stats_copy.wait_send()
        dq_copy.wait_send()


def on_device(
    q_raw,
    out_grad,
    q_gain,
    image_keys,
    image_values,
    block_images,
    image_slot,
    tile_counts,
    q_weight,
):
    rows, cols = q_raw.shape
    key_count = image_keys.shape[1]
    padded = -(-key_count // CHUNK) * CHUNK
    chunks = padded // CHUNK
    seq = lax.axis_index("seq")
    limit = jnp.sum(jnp.where(image_slot == seq, tile_counts, 0)).reshape(1) * TILE_TOK
    vmem = pl.BlockSpec(memory_space=pltpu.VMEM)
    V = pltpu.VMEM
    raw_grad, key_grad, value_grad = pl.pallas_call(
        attention_kernel,
        out_shape=(
            jax.ShapeDtypeStruct((rows, cols), bf16),
            jax.ShapeDtypeStruct(image_keys.shape, bf16),
            jax.ShapeDtypeStruct(image_values.shape, bf16),
        ),
        in_specs=[pl.BlockSpec(memory_space=pltpu.SMEM)] + [vmem] * 5,
        out_specs=(vmem, vmem, vmem),
        scratch_shapes=[
            V((padded, HD), bf16),
            V((padded, HD), bf16),
            V((HD, padded), bf16),
            V((HD + 16, padded), bf16),
            V((2, HD, cols), bf16),
            V((2, HD, cols), bf16),
            V((2, padded, cols), bf16),
            V((2, chunks, 8, cols), f32),
            V((HD + 16, cols), f32),
            V((HD, padded), f32),
            V((HD, padded), f32),
            V((HD, cols), f32),
            V((8, cols), f32),
            V((8, cols), f32),
            V((8, cols), f32),
            V((1, 8, cols), f32),
            V((8, cols), f32),
            V((HD, cols), bf16),
            V((HD, cols), bf16),
            pltpu.SemaphoreType.DMA((5,)),
            pltpu.SemaphoreType.DMA((5,)),
        ],
        compiler_params=pltpu.CompilerParams(
            collective_id=0, has_side_effects=True, vmem_limit_bytes=60 << 20
        ),
        name="attention",
    )(limit, q_raw, out_grad, q_gain.reshape(1, HD), image_keys, image_values)
    text_grad = lax.psum_scatter(
        lax.dot_general(
            raw_grad, q_weight, (((1,), (1,)), ((), ())), preferred_element_type=jnp.float32
        ).astype(jnp.bfloat16),
        "tp",
        scatter_dimension=0,
        tiled=True,
    )
    return (text_grad, key_grad, value_grad)


def solution(mesh):
    return jax.shard_map(
        on_device,
        mesh=mesh,
        in_specs=(
            P("seq", "tp"),
            P("seq", "tp"),
            P(),
            P("seq", None, "tp"),
            P("seq", None, "tp"),
            P(),
            P(),
            P(),
            P(None, "tp"),
        ),
        out_specs=(P(("seq", "tp"), None), P("seq", None, "tp"), P("seq", None, "tp")),
        check_vma=False,
    )
```

time: 596 us -> 145 us (0.24); the launches traced: 590 us -> 145 us
  matrix products: 268 us -> 12.8 us
  local copies, waits for them, and re-layouts: 136 us -> 2.34 us
  Pallas kernels: 0 us -> 81.7 us
  loops' own time: 61.7 us -> 0 us
  other arithmetic: 36.4 us -> 1.31 us
  starting transfers between devices: 20.9 us -> 0.04 us
  waiting for transfers between devices: 51.7 us -> 32.3 us
    dot_general x64 -> x0, matrix products: 255 us -> none  [the longest x40 173 us: key_product(): lax.dot_general(tile_data, query_cols, (((2,), (1,)), ((0,), (0,))), pref...]
    dynamic_update_slice x32 -> x0, local copies, waits for them, and re-layouts: 88 us -> none  [the longest x16 31.4 us: grad_step(): lax.dynamic_update_slice_in_dim(rows_grad, previous + query_part, row_sta...]
    pallas_call x0 -> x1, Pallas kernels: none -> 81.7 us  [on_device(): pl.pallas_call(attention_kernel, out_shape=(jax.ShapeDtypeStruct((rows, c...]
    another operation x3 -> x0, loops' own time: 61.7 us -> none  [the longest x2 41 us: sweep(): carry = lax.fori_loop(0, unit_total, partial(unit_step, 0, locate), carry)]
    dynamic_slice x32 -> x0, local copies, waits for them, and re-layouts: 32.4 us -> none  [the longest x16 16.6 us: grad_step(): previous = lax.dynamic_slice_in_dim(rows_grad, row_start, block_width, 2)]
    ppermute x7 -> x0, starting transfers between devices: 20.8 us -> none  [passed_along(): return lax.ppermute(x, axis, pairs)]
    ppermute x7 -> x0, waiting for transfers between devices: 16 us -> none  [passed_along(): return lax.ppermute(x, axis, pairs)]
    mul x25 -> x0, other arithmetic: 15.1 us -> none  [the longest x24 14.5 us: unit_data(): row_start = block_index * block_width]
  transfers between devices with their start and end apart: 8 -> 1, of which waited for: 7 -> 1; matrix products, arithmetic and copies ran while one was open for 7% -> 0% of each run, Pallas kernels for 0% -> 0%
where the time goes in v1:
time: 145 us
  Pallas kernels  81.7 us (56%)
  waiting for transfers between devices  32.3 us (22%)
  between operations  14.7 us (10%)
  matrix products  12.8 us (9%)
  local copies, waits for them, and re-layouts  2.34 us (2%)
    pallas_call x1, Pallas kernels, on_device(): pl.pallas_call(attention_kernel, out_shape=(jax.ShapeDtypeStruct((rows, c...  81.7 us
    reduce_scatter x1, waiting for transfers between devices, on_device(): lax.psum_scatter(lax.dot_general(raw_grad, q_weight, (((1,), (1,)), ((),...  32.3 us
    dot_general x1, matrix products, on_device(): lax.dot_general(raw_grad, q_weight, (((1,), (1,)), ((), ())), preferred_e...  12.8 us
  transfers between devices with their start and end apart: 1, of which 1 were waited for; matrix products, arithmetic and copies ran while one was open for 0% of the time, Pallas kernels for 0%

profile of v1, /device:TPU:0, one launch (start us, length us, event | category | flops | bytes accessed | tf_op | source)
XLA Modules:
  0.0 145.3 jit_solution(12994528085907826267)
XLA Ops:
  7.2 0.0 reduce-scatter.2.cloned.1.call-start
  7.2 1.3 fusion
  9.2 81.7 %attention.1 = (bf16[128,1024]{1,0:T(8,128)(2,1)}, bf16[1,6404,128]{2,1,0:T(8,128)(2,1)}, bf16[1,6404,128]{2,1,0:T(8,128)(2,1)}) custom-call(s32[1]{0:T(128)} %bitcast.limit_ref, bf16[128,1024]{1,0:T(8,128)(2,1)} %q_ref.1, bf16[128,1024]{1,0:T(8,128)(2,1)} %g_ref.1, f32[1,128]{1,0:T(1,128)} %bitcast.4, bf16[1,6404,128]{2,1,0:T(8,128)(2,1)} %key_ref.1, ...), custom_call_target="tpu_custom_call" | custom-call | tf_op jit(solution)/shard_map/attention/pallas_call | solution.py:318
  90.9 12.8 %convolution_convert_fusion = bf16[128,8192]{1,0:T(8,128)(2,1)} fusion(bf16[128,1024]{1,0:T(8,128)(2,1)} %get-tuple-element.6, bf16[8192,1024]{1,0:T(8,128)(2,1)} %param.16), kind=kOutput, calls=%fused_computation | convolution fusion | flops 2148532224 | bytes 19136512 | tf_op jit(solution)/shard_map/dot_general | solution.py:356
  103.7 0.0 copy-start.1
  103.7 0.0 reduce-scatter.2.cloned.1.call-update
  103.8 0.0 copy-start
  103.8 32.3 %reduce-scatter.2.cloned.1.call-done = bf16[16,8192]{1,0:T(8,128)(2,1)} async-done(((bf16[128,8192]{1,0:T(8,128)(2,1)}), bf16[16,8192]{1,0:T(8,128)(2,1)}) %reduce-scatter.2.cloned.1.call-update) | async-done | bytes 262160 | tf_op jit(solution)/shard_map/reduce_scatter | solution.py:355
  136.1 0.0 copy-done.1
  136.1 1.2 copy.13
  137.2 0.0 copy-done
  137.2 1.2 copy.14
Async XLA Ops:
  7.2 128.9 %reduce-scatter.2.cloned.1.call-start = ((), (), s32[]{:S(2)}) async-start(), calls=%async_computation.1 | async-start | bytes 2359296 | tf_op jit(solution)/shard_map/reduce_scatter | solution.py:355
  103.7 32.3 %copy-start.1 = (bf16[1,6404,128]{2,1,0:T(8,128)(2,1)S(1)}, bf16[1,6404,128]{2,1,0:T(8,128)(2,1)}, u32[]{:S(2)}) copy-start(bf16[1,6404,128]{2,1,0:T(8,128)(2,1)} %get-tuple-element.13) | copy-start | bytes 4918276
  103.8 33.5 %copy-start = (bf16[1,6404,128]{2,1,0:T(8,128)(2,1)S(1)}, bf16[1,6404,128]{2,1,0:T(8,128)(2,1)}, u32[]{:S(2)}) copy-start(bf16[1,6404,128]{2,1,0:T(8,128)(2,1)} %get-tuple-element.14) | copy-start | bytes 4918276
Sparse Core Ops, SparseCore 0:
  103.9 32.1 reduce-scatter.1

commit v2 on v1

--- a/solution.py
+++ b/solution.py
@@ -12,6 +12,7 @@
 TILE_TOK = 1601
 CHUNK = 512
 GROUP = 256
+PARTS = 8
 norm_eps = 1e-05
 score_scale = 1.0 / math.sqrt(HD)
 exp2_scale = score_scale * math.log2(math.e)
@@ -34,7 +35,8 @@
     gain_ref,
     key_ref,
     value_ref,
-    raw_out,
+    weight_ref,
+    text_out,
     key_out,
     value_out,
     keys,
@@ -56,8 +58,20 @@
     total_in,
     dq_send,
     dq_in,
+    raw_low,
+    weight_tail,
+    kept,
+    pair_send,
+    pair_in,
+    far_send,
+    far_in,
+    near_send,
+    near_in,
+    weight_sem,
     send_sem,
     recv_sem,
+    part_send_sem,
+    part_recv_sem,
 ):
     seq = lax.axis_index("seq")
     tp = lax.axis_index("tp")
@@ -76,8 +90,14 @@
 
     barrier = pltpu.get_barrier_semaphore()
 
-    for step in (1, seq_size - 1):
-        near = (lax.rem(seq + step, seq_size), tp)
+    chips = lax.axis_size("tp") // 2
+    chip, core = lax.div(tp, 2), lax.rem(tp, 2)
+    pair = (seq, tp + 1 - 2 * core)
+    up_chip, down_chip = lax.rem(chip + 1, chips), lax.rem(chip + chips - 1, chips)
+    far_chip = lax.rem(chip + 2, chips)
+    up, down = (seq, up_chip * 2 + core), (seq, down_chip * 2 + core)
+    ahead, behind = lax.rem(seq + 1, seq_size), lax.rem(seq + seq_size - 1, seq_size)
+    for near in ((ahead, tp), (behind, tp), pair, up, down):
         pl.semaphore_signal(barrier, inc=1, device_id=near, device_id_type=MESH)
 
     def rdma(index, src, dst, device):
@@ -96,6 +116,16 @@
     total_copy = rdma(3, total.at[0], total_in, left)
     dq_copy = rdma(4, dq_send, dq_in, right)
 
+    width = weight_ref.shape[0] // PARTS
+    early = (padded // width) * width
+    weight_copies = (
+        pltpu.make_async_copy(
+            weight_ref.at[0:early], e_all.at[1, 0:early], weight_sem.at[0]
+        ),
+        pltpu.make_async_copy(weight_ref.at[early:], weight_tail, weight_sem.at[1]),
+    )
+    weight_copies[1].start()
+
     gain = gain_ref[...]
     for h in range(heads):
         span = slice(h * HD, (h + 1) * HD)
@@ -105,7 +135,7 @@
         qt[0, :, span] = normed.T.astype(bf16)
         gt[0, :, span] = g_ref[:, span].T
 
-    pl.semaphore_wait(barrier, 2)
+    pl.semaphore_wait(barrier, 5)
 
     @pl.when(has_left)
     def _():
@@ -253,6 +283,7 @@
         dkt[...] = jnp.zeros_like(dkt)
         dvt[...] = jnp.zeros_like(dvt)
 
+    weight_copies[0].start()
     grads_pass(0, total.at[0], emit)
 
     def output(start, rows):
@@ -282,7 +313,81 @@
         inv = lax.rsqrt(jnp.mean(raw * raw, axis=-1, keepdims=True) + norm_eps)
         scaled = dqt[:, span].T * score_scale * gain
         spread = jnp.mean(scaled * raw, axis=-1, keepdims=True)
-        raw_out[:, span] = (inv * scaled - raw * (inv * inv * inv) * spread).astype(bf16)
+        raw_low[:, span] = (inv * scaled - raw * (inv * inv * inv) * spread).astype(bf16)
+
+    half = width // 2
+
+    def part_copy(kind, n, src, dst, device):
+        return pltpu.make_async_remote_copy(
+            src_ref=src,
+            dst_ref=dst,
+            send_sem=part_send_sem.at[kind, n],
+            recv_sem=part_recv_sem.at[kind, n],
+            device_id=device,
+            device_id_type=MESH,
+        )
+
+    def pair_copy(n):
+        return part_copy(0, n, pair_send.at[n], pair_in.at[n], pair)
+
+    def far_copies(n):
+        return (
+            part_copy(1, n, far_send.at[0, n], far_in.at[0, n], up),
+            part_copy(2, n, far_send.at[1, n], far_in.at[1, n], down),
+        )
+
+    def near_copies(n):
+        return (
+            part_copy(3, n, near_send.at[0, n], near_in.at[0, n], up),
+            part_copy(4, n, near_send.at[1, n], near_in.at[1, n], down),
+        )
+
+    def multiply(n):
+        if (n + 1) * width <= early:
+            rows = e_all[1, n * width : (n + 1) * width, :]
+        else:
+            rows = weight_tail[n * width - early : (n + 1) * width - early, :]
+        product = nt(raw_low[...], rows).reshape(chips, 2, 16, width)
+        first, second = product[:, 0], product[:, 1]
+        kept[n] = jnp.where(core == 0, first, second)
+        pair_send[n] = jnp.where(core == 0, second, first).astype(bf16)
+        pair_copy(n).start()
+
+    def send_far(n):
+        pair_copy(n).wait_recv()
+        kept[n] = kept[n] + pair_in[n].astype(f32)
+        far = kept[n, far_chip].astype(bf16)
+        far_send[0, n] = far[:, 0:half]
+        far_send[1, n] = far[:, half:width]
+        for copy in far_copies(n):
+            copy.start()
+
+    def send_near(n):
+        for copy in far_copies(n):
+            copy.wait_recv()
+        one, other = kept[n, up_chip], kept[n, down_chip]
+        near_send[0, n, :, 0:half] = (one[:, 0:half] + far_in[0, n].astype(f32)).astype(bf16)
+        near_send[0, n, :, half:width] = one[:, half:width].astype(bf16)
+        near_send[1, n, :, 0:half] = other[:, 0:half].astype(bf16)
+        near_send[1, n, :, half:width] = (other[:, half:width] + far_in[1, n].astype(f32)).astype(bf16)
+        for copy in near_copies(n):
+            copy.start()
+
+    def finish(n):
+        for copy in near_copies(n):
+            copy.wait_recv()
+        whole_sum = kept[n, chip] + near_in[0, n].astype(f32) + near_in[1, n].astype(f32)
+        text_out[:, n * width : (n + 1) * width] = whole_sum.astype(bf16)
+
+    for copy in weight_copies:
+        copy.wait()
+    for t in range(PARTS + 10):
+        for lag, stage in ((0, multiply), (3, send_far), (6, send_near), (10, finish)):
+            if 0 <= t - lag < PARTS:
+                stage(t - lag)
+    for n in range(PARTS):
+        for copy in (pair_copy(n), *far_copies(n), *near_copies(n)):
+            copy.wait_send()
 
     @pl.when(has_left)
     def _():
@@ -315,14 +420,17 @@
     limit = jnp.sum(jnp.where(image_slot == seq, tile_counts, 0)).reshape(1) * TILE_TOK
     vmem = pl.BlockSpec(memory_space=pltpu.VMEM)
     V = pltpu.VMEM
-    raw_grad, key_grad, value_grad = pl.pallas_call(
+    width = q_weight.shape[0] // PARTS
+    weight_rest = q_weight.shape[0] - padded // width * width
+    chips = lax.axis_size("tp") // 2
+    return pl.pallas_call(
         attention_kernel,
         out_shape=(
-            jax.ShapeDtypeStruct((rows, cols), bf16),
+            jax.ShapeDtypeStruct((rows // (2 * chips), q_weight.shape[0]), bf16),
             jax.ShapeDtypeStruct(image_keys.shape, bf16),
             jax.ShapeDtypeStruct(image_values.shape, bf16),
         ),
-        in_specs=[pl.BlockSpec(memory_space=pltpu.SMEM)] + [vmem] * 5,
+        in_specs=[pl.BlockSpec(memory_space=pltpu.SMEM)] + [vmem] * 5 + [pl.BlockSpec(memory_space=pl.ANY)],
         out_specs=(vmem, vmem, vmem),
         scratch_shapes=[
             V((padded, HD), bf16),
@@ -332,7 +440,7 @@
             V((2, HD, cols), bf16),
             V((2, HD, cols), bf16),
             V((2, padded, cols), bf16),
-            V((2, chunks, 8, cols), f32),
+            V((2, chunks, 1, cols), f32),
             V((HD + 16, cols), f32),
             V((HD, padded), f32),
             V((HD, padded), f32),
@@ -344,23 +452,26 @@
             V((8, cols), f32),
             V((HD, cols), bf16),
             V((HD, cols), bf16),
+            V((rows, cols), bf16),
+            V((weight_rest, cols), bf16),
+            V((PARTS, chips, 16, width), f32),
+            V((PARTS, chips, 16, width), bf16),
+            V((PARTS, chips, 16, width), bf16),
+            V((2, PARTS, 16, width // 2), bf16),
+            V((2, PARTS, 16, width // 2), bf16),
+            V((2, PARTS, 16, width), bf16),
+            V((2, PARTS, 16, width), bf16),
+            pltpu.SemaphoreType.DMA((2,)),
             pltpu.SemaphoreType.DMA((5,)),
             pltpu.SemaphoreType.DMA((5,)),
+            pltpu.SemaphoreType.DMA((5, PARTS)),
+            pltpu.SemaphoreType.DMA((5, PARTS)),
         ],
         compiler_params=pltpu.CompilerParams(
-            collective_id=0, has_side_effects=True, vmem_limit_bytes=60 << 20
+            collective_id=0, has_side_effects=True, vmem_limit_bytes=63 << 20
         ),
         name="attention",
-    )(limit, q_raw, out_grad, q_gain.reshape(1, HD), image_keys, image_values)
-    text_grad = lax.psum_scatter(
-        lax.dot_general(
-            raw_grad, q_weight, (((1,), (1,)), ((), ())), preferred_element_type=jnp.float32
-        ).astype(jnp.bfloat16),
-        "tp",
-        scatter_dimension=0,
-        tiled=True,
-    )
-    return (text_grad, key_grad, value_grad)
+    )(limit, q_raw, out_grad, q_gain.reshape(1, HD), image_keys, image_values, q_weight)
 
 
 def solution(mesh):

time: 145 us -> 109 us (0.75)
  waiting for transfers between devices: 32.3 us -> 0 us
  Pallas kernels: 81.7 us -> 101 us
  between operations: 14.7 us -> 1.3 us
  matrix products: 12.8 us -> 0 us
  local copies, waits for them, and re-layouts: 2.34 us -> 5.66 us
    reduce_scatter x1 -> x0, waiting for transfers between devices: 32.3 us -> none  [on_device(): lax.psum_scatter(lax.dot_general(raw_grad, q_weight, (((1,), (1,)), ((),...]
    pallas_call x1, Pallas kernels: 81.7 us -> 101 us  [on_device(): pl.pallas_call(attention_kernel, out_shape=(jax.ShapeDtypeStruct((rows //...]
    dot_general x1 -> x0, matrix products: 12.8 us -> none  [on_device(): lax.dot_general(raw_grad, q_weight, (((1,), (1,)), ((), ())), preferred_e...]
    unnamed x6 -> x5, local copies, waits for them, and re-layouts: 2.34 us -> 5.66 us
  transfers between devices with their start and end apart: 1 -> 0, of which waited for: 1 -> 0; matrix products, arithmetic and copies ran while one was open for 0% -> 0% of each run, Pallas kernels for 0% -> 0%
where the time goes in v2:
time: 109 us
  Pallas kernels  101 us (93%)
  local copies, waits for them, and re-layouts  5.66 us (5%)
  other arithmetic  1.31 us (1%)
  between operations  1.3 us (1%)
    pallas_call x1, Pallas kernels, on_device(): pl.pallas_call(attention_kernel, out_shape=(jax.ShapeDtypeStruct((rows //...  101 us
    unnamed x5, local copies, waits for them, and re-layouts  5.66 us

profile of v2, /device:TPU:0, one launch (start us, length us, event | category | flops | bytes accessed | tf_op | source)
XLA Modules:
  0.0 109.3 jit_solution(8009109968628107588)
XLA Ops:
  0.6 1.3 %fusion = s32[]{:T(128)} fusion(s32[16]{0:T(128)} %param.15, s32[16]{0:T(128)} %param.14, s32[]{:T(128)S(6)} %axis_index.15), kind=kLoop, calls=%fused_computation.1 | loop fusion | flops 47 | bytes 136 | tf_op jit(solution)/shard_map/reduce_sum | solution.py:420
  2.6 101.0 %attention.1 = (bf16[16,8192]{1,0:T(8,128)(2,1)}, bf16[1,6404,128]{2,1,0:T(8,128)(2,1)}, bf16[1,6404,128]{2,1,0:T(8,128)(2,1)}) custom-call(s32[1]{0:T(128)} %bitcast.limit_ref, bf16[128,1024]{1,0:T(8,128)(2,1)} %q_ref.1, bf16[128,1024]{1,0:T(8,128)(2,1)} %g_ref.1, f32[1,128]{1,0:T(1,128)} %bitcast.2, bf16[1,6404,128]{2,1,0:T(8,128)(2,1)} %key_ref.1, ...), custom_call_target="tpu_custom_call" | custom-call | tf_op jit(solution)/shard_map/attention/pallas_call | solution.py:426
  103.6 1.7 %copy.14 = bf16[16,8192]{1,0:T(8,128)(2,1)} copy(bf16[16,8192]{1,0:T(8,128)(2,1)} %get-tuple-element.6) | data formatting | bytes 524288
  105.3 0.0 copy-start
  105.3 2.8 %copy.15 = bf16[1,6404,128]{2,1,0:T(8,128)(2,1)} copy(bf16[1,6404,128]{2,1,0:T(8,128)(2,1)} %get-tuple-element.7) | data formatting | bytes 3278848
  108.1 0.0 copy-done
  108.1 1.2 %copy.16 = bf16[1,6404,128]{2,1,0:T(8,128)(2,1)} copy(bf16[1,6404,128]{2,1,0:T(8,128)(2,1)S(1)} %copy-done) | data formatting | bytes 3278848
Async XLA Ops:
  105.3 2.8 %copy-start = (bf16[1,6404,128]{2,1,0:T(8,128)(2,1)S(1)}, bf16[1,6404,128]{2,1,0:T(8,128)(2,1)}, u32[]{:S(2)}) copy-start(bf16[1,6404,128]{2,1,0:T(8,128)(2,1)} %get-tuple-element.8) | copy-start | bytes 4918276

commit v3 on v2

--- a/solution.py
+++ b/solution.py
@@ -29,7 +29,8 @@
 
 
 def attention_kernel(
-    limit_ref,
+    slot_ref,
+    tiles_ref,
     q_ref,
     g_ref,
     gain_ref,
@@ -39,6 +40,8 @@
     text_out,
     key_out,
     value_out,
+    key_rows_ref,
+    value_rows_ref,
     keys,
     values,
     keys_t,
@@ -47,6 +50,9 @@
     gt,
     e_all,
     m_all,
+    held,
+    probs_t,
+    grads_t,
     acc,
     dkt,
     dvt,
@@ -60,14 +66,13 @@
     dq_in,
     raw_low,
     weight_tail,
-    kept,
     pair_send,
     pair_in,
     far_send,
     far_in,
     near_send,
     near_in,
-    weight_sem,
+    local_sem,
     send_sem,
     recv_sem,
     part_send_sem,
@@ -86,7 +91,10 @@
     padded = keys.shape[0]
     chunks = padded // CHUNK
     groups = cols // GROUP
-    limit = limit_ref[0]
+    limit = jnp.int32(0)
+    for i in range(slot_ref.shape[0]):
+        limit += jnp.where(slot_ref[i] == seq, tiles_ref[i], 0)
+    limit = limit * TILE_TOK
 
     barrier = pltpu.get_barrier_semaphore()
 
@@ -120,10 +128,20 @@
     early = (padded // width) * width
     weight_copies = (
         pltpu.make_async_copy(
-            weight_ref.at[0:early], e_all.at[1, 0:early], weight_sem.at[0]
+            weight_ref.at[0:early], e_all.at[1, 0:early], local_sem.at[0]
         ),
-        pltpu.make_async_copy(weight_ref.at[early:], weight_tail, weight_sem.at[1]),
+        pltpu.make_async_copy(weight_ref.at[early:], weight_tail, local_sem.at[1]),
     )
+    row_copies = (
+        pltpu.make_async_copy(key_ref.at[0], key_rows_ref, local_sem.at[2]),
+        pltpu.make_async_copy(value_ref.at[0], value_rows_ref, local_sem.at[3]),
+    )
+    out_copies = (
+        pltpu.make_async_copy(key_rows_ref, key_out.at[0], local_sem.at[4]),
+        pltpu.make_async_copy(value_rows_ref, value_out.at[0], local_sem.at[5]),
+    )
+    for copy in row_copies:
+        copy.start()
     weight_copies[1].start()
 
     gain = gain_ref[...]
@@ -133,16 +151,19 @@
         inv = lax.rsqrt(jnp.mean(raw * raw, axis=-1, keepdims=True) + norm_eps)
         normed = raw * inv * gain
         qt[0, :, span] = normed.T.astype(bf16)
+
+    pl.semaphore_wait(barrier, 5)
+
+    @pl.when(has_left)
+    def _():
+        q_copy.start()
+
+    for h in range(heads):
+        span = slice(h * HD, (h + 1) * HD)
         gt[0, :, span] = g_ref[:, span].T
-
-    pl.semaphore_wait(barrier, 5)
-
-    @pl.when(has_left)
-    def _():
-        q_copy.start()
-        g_copy.start()
-
-    first_key = key_ref[0, 0:1, :]
+    for copy in row_copies:
+        copy.wait()
+    first_key = key_rows_ref[0:1, :]
 
     def fill(start, rows, key_rows, value_rows):
         held = key_rows.shape[0]
@@ -161,50 +182,70 @@
         live_t = start + lax.broadcasted_iota(jnp.int32, (16, rows), 1) < limit
         values_t[HD : HD + 16, pl.ds(start, rows)] = jnp.where(live_t, 1.0, 0.0).astype(bf16)
 
-    def fill_step(i, carry):
+    def fill_chunk(i):
         start = pl.multiple_of(i * CHUNK, CHUNK)
-        fill(start, CHUNK, key_ref[0, pl.ds(start, CHUNK), :], value_ref[0, pl.ds(start, CHUNK), :])
-        return carry
+        span = pl.ds(start, CHUNK)
+        fill(start, CHUNK, key_rows_ref[span, :], value_rows_ref[span, :])
 
     whole = key_count // CHUNK
-    lax.fori_loop(0, whole, fill_step, 0)
     if whole < chunks:
         tail = whole * CHUNK
-        fill(tail, CHUNK, key_ref[0, tail:key_count, :], value_ref[0, tail:key_count, :])
+        fill(tail, CHUNK, key_rows_ref[tail:key_count, :], value_rows_ref[tail:key_count, :])
+    fill_chunk(0)
+    fill_chunk(1)
+
+    def columns(j):
+        return slice(j * GROUP, (j + 1) * GROUP)
+
+    def chunk_start(i):
+        return pl.multiple_of(i * CHUNK, CHUNK)
 
     def totals_pass(b, stats):
+        def scores_of(start, j):
+            return nn(keys[pl.ds(start, CHUNK), :], qt[b, :, columns(j)])
+
+        for j in range(groups):
+            first = scores_of(0, j)
+            held[:, columns(j)] = first
+            stats[0:1, columns(j)] = jnp.max(first, axis=0, keepdims=True) * exp2_scale
+        stats[1:2, :] = stats[0:1, :]
         acc[...] = jnp.zeros_like(acc)
-        stats[0:1, :] = jnp.full((1, cols), -1e30, f32)
-
-        def step(i, carry):
-            start = pl.multiple_of(i * CHUNK, CHUNK)
-            key_chunk = keys[pl.ds(start, CHUNK), :]
+
+        def step(i, carry, last=False):
+            start = chunk_start(i)
             value_chunk = values_t[:, pl.ds(start, CHUNK)]
-
-            def product(j):
-                return nn(key_chunk, qt[b, :, j * GROUP : (j + 1) * GROUP])
-
-            scores = product(0)
+            if b == 0 and not last:
+                fill_chunk(jnp.minimum(i + 2, whole - 1))
             for j in range(groups):
-                later = product(j + 1) if j + 1 < groups else None
-                span = slice(j * GROUP, (j + 1) * GROUP)
-                before = stats[0:1, span]
-                top = jnp.maximum(before, jnp.max(scores, axis=0, keepdims=True) * exp2_scale)
-                stats[0:1, span] = top
+                span = columns(j)
+                top = stats[0:1, span]
+                before = stats[1:2, span]
+                low = jnp.exp2(held[:, span] * exp2_scale - top).astype(bf16)
                 m_all[b, i, 0:1, span] = top
-                low = jnp.exp2(scores * exp2_scale - top).astype(bf16)
                 e_all[b, pl.ds(start, CHUNK), span] = low
+                if not last:
+                    later = scores_of(chunk_start(i + 1), j)
+                    held[:, span] = later
+                    stats[0:1, span] = jnp.maximum(
+                        top, jnp.max(later, axis=0, keepdims=True) * exp2_scale
+                    )
+                    stats[1:2, span] = top
                 acc[:, span] = acc[:, span] * jnp.exp2(before - top) + nn(value_chunk, low)
-                scores = later
             return carry
 
-        lax.fori_loop(0, chunks, step, 0)
+        lax.fori_loop(0, chunks - 1, step, 0)
+        step(chunks - 1, 0, True)
         stats[1:2, :] = acc[HD : HD + 1, :]
 
     def finish_totals(b, stats):
         stats[2:3, :] = jnp.sum(acc[0:HD, :] * gt[b].astype(f32), axis=0, keepdims=True)
 
     totals_pass(0, stats_own)
+
+    @pl.when(has_left)
+    def _():
+        g_copy.start()
+
     finish_totals(0, stats_own)
 
     @pl.when(has_next)
@@ -234,35 +275,37 @@
         total[0, 1:2, :] = stats_own[2:3, :] / norm
 
     def grads_pass(b, totals, write):
+        def slopes_of(start, j):
+            return nn(values[pl.ds(start, CHUNK), :], gt[b, :, columns(j)])
+
+        for j in range(groups):
+            held[:, columns(j)] = slopes_of(0, j)
         dqt[...] = jnp.zeros_like(dqt)
 
-        def step(i, carry):
-            start = pl.multiple_of(i * CHUNK, CHUNK)
-            value_chunk = values[pl.ds(start, CHUNK), :]
+        def step(i, carry, last=False):
+            start = chunk_start(i)
             key_chunk = keys_t[:, pl.ds(start, CHUNK)]
-
-            def product(j):
-                return nn(value_chunk, gt[b, :, j * GROUP : (j + 1) * GROUP])
-
-            slopes = product(0)
             key_part, value_part = None, None
             for j in range(groups):
-                later = product(j + 1) if j + 1 < groups else None
-                span = slice(j * GROUP, (j + 1) * GROUP)
+                span = columns(j)
                 weight = jnp.exp2(m_all[b, i, 0:1, span] - totals[0:1, span])
                 probs = e_all[b, pl.ds(start, CHUNK), span].astype(f32) * weight
                 probs_low = probs.astype(bf16)
-                score_grad = (probs * (slopes - totals[1:2, span])).astype(bf16)
-                v_part = nt(gt[b, :, span], probs_low)
-                k_part = nt(qt[b, :, span], score_grad)
+                score_grad = (probs * (held[:, span] - totals[1:2, span])).astype(bf16)
+                if not last:
+                    held[:, span] = slopes_of(chunk_start(i + 1), j)
+                probs_t[span, :] = probs_low.T
+                grads_t[span, :] = score_grad.T
+                v_part = nn(gt[b, :, span], probs_t[span, :])
+                k_part = nn(qt[b, :, span], grads_t[span, :])
                 dqt[:, span] += nn(key_chunk, score_grad)
                 key_part = k_part if j == 0 else key_part + k_part
                 value_part = v_part if j == 0 else value_part + v_part
-                slopes = later
             write(start, key_part, value_part)
             return carry
 
-        lax.fori_loop(0, chunks, step, 0)
+        lax.fori_loop(0, chunks - 1, step, 0)
+        step(chunks - 1, 0, True)
 
     def hold(start, key_part, value_part):
         dkt[:, pl.ds(start, CHUNK)] = key_part
@@ -286,21 +329,18 @@
     weight_copies[0].start()
     grads_pass(0, total.at[0], emit)
 
-    def output(start, rows):
+    def output(i):
+        start = i * CHUNK
+        rows = min(CHUNK, key_count - start)
         live = start + lax.broadcasted_iota(jnp.int32, (rows, HD), 0) < limit
-        span = pl.ds(start, CHUNK)
+        span = slice(start, start + CHUNK)
         key_rows = (dkt[:, span] * score_scale).T[0:rows]
         value_rows = dvt[:, span].T[0:rows]
-        key_out[0, pl.ds(start, rows), :] = jnp.where(live, key_rows, 0.0).astype(bf16)
-        value_out[0, pl.ds(start, rows), :] = jnp.where(live, value_rows, 0.0).astype(bf16)
-
-    def output_step(i, carry):
-        output(pl.multiple_of(i * CHUNK, CHUNK), CHUNK)
-        return carry
-
-    lax.fori_loop(0, whole, output_step, 0)
-    if whole < chunks:
-        output(whole * CHUNK, key_count - whole * CHUNK)
+        key_rows_ref[start : start + rows, :] = jnp.where(live, key_rows, 0.0).astype(bf16)
+        value_rows_ref[start : start + rows, :] = jnp.where(live, value_rows, 0.0).astype(bf16)
+        if i == chunks - 1:
+            for copy in out_copies:
+                copy.start()
 
     @pl.when(has_left)
     def _():
@@ -342,6 +382,9 @@
             part_copy(4, n, near_send.at[1, n], near_in.at[1, n], down),
         )
 
+    def kept(n, place):
+        return pl.ds(pl.multiple_of((n * chips + place) * 16, 16), 16)
+
     def multiply(n):
         if (n + 1) * width <= early:
             rows = e_all[1, n * width : (n + 1) * width, :]
@@ -349,14 +392,18 @@
             rows = weight_tail[n * width - early : (n + 1) * width - early, :]
         product = nt(raw_low[...], rows).reshape(chips, 2, 16, width)
         first, second = product[:, 0], product[:, 1]
-        kept[n] = jnp.where(core == 0, first, second)
+        held[n * chips * 16 : (n + 1) * chips * 16, :] = jnp.where(
+            core == 0, first, second
+        ).reshape(chips * 16, width)
         pair_send[n] = jnp.where(core == 0, second, first).astype(bf16)
         pair_copy(n).start()
 
     def send_far(n):
         pair_copy(n).wait_recv()
-        kept[n] = kept[n] + pair_in[n].astype(f32)
-        far = kept[n, far_chip].astype(bf16)
+        held[n * chips * 16 : (n + 1) * chips * 16, :] += (
+            pair_in[n].astype(f32).reshape(chips * 16, width)
+        )
+        far = held[kept(n, far_chip), :].astype(bf16)
         far_send[0, n] = far[:, 0:half]
         far_send[1, n] = far[:, half:width]
         for copy in far_copies(n):
@@ -365,7 +412,7 @@
     def send_near(n):
         for copy in far_copies(n):
             copy.wait_recv()
-        one, other = kept[n, up_chip], kept[n, down_chip]
+        one, other = held[kept(n, up_chip), :], held[kept(n, down_chip), :]
         near_send[0, n, :, 0:half] = (one[:, 0:half] + far_in[0, n].astype(f32)).astype(bf16)
         near_send[0, n, :, half:width] = one[:, half:width].astype(bf16)
         near_send[1, n, :, 0:half] = other[:, 0:half].astype(bf16)
@@ -376,7 +423,7 @@
     def finish(n):
         for copy in near_copies(n):
             copy.wait_recv()
-        whole_sum = kept[n, chip] + near_in[0, n].astype(f32) + near_in[1, n].astype(f32)
+        whole_sum = held[kept(n, chip), :] + near_in[0, n].astype(f32) + near_in[1, n].astype(f32)
         text_out[:, n * width : (n + 1) * width] = whole_sum.astype(bf16)
 
     for copy in weight_copies:
@@ -385,6 +432,10 @@
         for lag, stage in ((0, multiply), (3, send_far), (6, send_near), (10, finish)):
             if 0 <= t - lag < PARTS:
                 stage(t - lag)
+        if 3 <= t < chunks + 3:
+            output(t - 3)
+    for copy in out_copies:
+        copy.wait()
     for n in range(PARTS):
         for copy in (pair_copy(n), *far_copies(n), *near_copies(n)):
             copy.wait_send()
@@ -399,6 +450,27 @@
     def _():
         stats_copy.wait_send()
         dq_copy.wait_send()
+
+
+def hand_over_kernel(
+    text_in, key_in, value_in, text_out, key_out, value_out, text, keys, values, in_sem, out_sem
+):
+    held = (text, keys, values)
+    arrive = [
+        pltpu.make_async_copy(src, dst, in_sem.at[n])
+        for n, (src, dst) in enumerate(zip((text_in, key_in, value_in), held))
+    ]
+    leave = [
+        pltpu.make_async_copy(src, dst, out_sem.at[n])
+        for n, (src, dst) in enumerate(zip(held, (text_out, key_out, value_out)))
+    ]
+    for copy in arrive:
+        copy.start()
+    for first, second in zip(arrive, leave):
+        first.wait()
+        second.start()
+    for copy in leave:
+        copy.wait()
 
 
 def on_device(
@@ -416,23 +488,25 @@
     key_count = image_keys.shape[1]
     padded = -(-key_count // CHUNK) * CHUNK
     chunks = padded // CHUNK
-    seq = lax.axis_index("seq")
-    limit = jnp.sum(jnp.where(image_slot == seq, tile_counts, 0)).reshape(1) * TILE_TOK
+    smem = pl.BlockSpec(memory_space=pltpu.SMEM)
     vmem = pl.BlockSpec(memory_space=pltpu.VMEM)
+    hbm = pl.BlockSpec(memory_space=pl.ANY)
     V = pltpu.VMEM
     width = q_weight.shape[0] // PARTS
     weight_rest = q_weight.shape[0] - padded // width * width
     chips = lax.axis_size("tp") // 2
-    return pl.pallas_call(
+    results = pl.pallas_call(
         attention_kernel,
         out_shape=(
             jax.ShapeDtypeStruct((rows // (2 * chips), q_weight.shape[0]), bf16),
             jax.ShapeDtypeStruct(image_keys.shape, bf16),
             jax.ShapeDtypeStruct(image_values.shape, bf16),
         ),
-        in_specs=[pl.BlockSpec(memory_space=pltpu.SMEM)] + [vmem] * 5 + [pl.BlockSpec(memory_space=pl.ANY)],
-        out_specs=(vmem, vmem, vmem),
+        in_specs=[smem] * 2 + [vmem] * 3 + [hbm] * 3,
+        out_specs=(vmem, hbm, hbm),
         scratch_shapes=[
+            V((key_count, HD), bf16),
+            V((key_count, HD), bf16),
             V((padded, HD), bf16),
             V((padded, HD), bf16),
             V((HD, padded), bf16),
@@ -441,6 +515,9 @@
             V((2, HD, cols), bf16),
             V((2, padded, cols), bf16),
             V((2, chunks, 1, cols), f32),
+            V((CHUNK, cols), f32),
+            V((cols, CHUNK), bf16),
+            V((cols, CHUNK), bf16),
             V((HD + 16, cols), f32),
             V((HD, padded), f32),
             V((HD, padded), f32),
@@ -454,14 +531,13 @@
             V((HD, cols), bf16),
             V((rows, cols), bf16),
             V((weight_rest, cols), bf16),
-            V((PARTS, chips, 16, width), f32),
             V((PARTS, chips, 16, width), bf16),
             V((PARTS, chips, 16, width), bf16),
             V((2, PARTS, 16, width // 2), bf16),
             V((2, PARTS, 16, width // 2), bf16),
             V((2, PARTS, 16, width), bf16),
             V((2, PARTS, 16, width), bf16),
-            pltpu.SemaphoreType.DMA((2,)),
+            pltpu.SemaphoreType.DMA((6,)),
             pltpu.SemaphoreType.DMA((5,)),
             pltpu.SemaphoreType.DMA((5,)),
             pltpu.SemaphoreType.DMA((5, PARTS)),
@@ -471,7 +547,17 @@
             collective_id=0, has_side_effects=True, vmem_limit_bytes=63 << 20
         ),
         name="attention",
-    )(limit, q_raw, out_grad, q_gain.reshape(1, HD), image_keys, image_values, q_weight)
+    )(image_slot, tile_counts, q_raw, out_grad, q_gain.reshape(1, HD), image_keys, image_values, q_weight)
+    return pl.pallas_call(
+        hand_over_kernel,
+        out_shape=tuple(jax.ShapeDtypeStruct(x.shape, x.dtype) for x in results),
+        in_specs=[hbm] * 3,
+        out_specs=(hbm, hbm, hbm),
+        scratch_shapes=[V(x.shape, x.dtype) for x in results]
+        + [pltpu.SemaphoreType.DMA((3,))] * 2,
+        compiler_params=pltpu.CompilerParams(vmem_limit_bytes=63 << 20),
+        name="hand_over",
+    )(*results)
 
 
 def solution(mesh):

time: 109 us -> 86 us (0.79)
  Pallas kernels: 101 us -> 85.1 us
  local copies, waits for them, and re-layouts: 5.66 us -> 0 us
  other arithmetic: 1.31 us -> 0 us
    pallas_call x1, Pallas kernels: 101 us -> 81.8 us  [on_device(): pl.pallas_call(attention_kernel, out_shape=(jax.ShapeDtypeStruct((rows //...]
    unnamed x5 -> x0, local copies, waits for them, and re-layouts: 5.66 us -> none
    pallas_call x0 -> x1, Pallas kernels: none -> 3.33 us  [on_device(): pl.pallas_call(hand_over_kernel, out_shape=tuple((jax.ShapeDtypeStruct(x....]
    reduce_sum x1 -> x0, other arithmetic: 1.31 us -> none  [on_device(): jnp.sum(jnp.where(image_slot == seq, tile_counts, 0)).reshape(1) * TILE_TOK]
where the time goes in v3:
time: 86 us; the launch traced here: 85.9 us
  Pallas kernels  85.1 us (99%)
    pallas_call x1, Pallas kernels, on_device(): pl.pallas_call(attention_kernel, out_shape=(jax.ShapeDtypeStruct((rows //...  81.8 us
    pallas_call x1, Pallas kernels, on_device(): pl.pallas_call(hand_over_kernel, out_shape=tuple((jax.ShapeDtypeStruct(x....  3.33 us

profile of v3, /device:TPU:0, one launch (start us, length us, event | category | flops | bytes accessed | tf_op | source)
XLA Modules:
  0.0 85.9 jit_solution(12596933476844933482)
XLA Ops:
  0.6 81.8 %attention.1 = (bf16[16,8192]{1,0:T(8,128)(2,1)}, bf16[1,6404,128]{2,1,0:T(8,128)(2,1)}, bf16[1,6404,128]{2,1,0:T(8,128)(2,1)}) custom-call(s32[16]{0:T(128)} %slot_ref.1, s32[16]{0:T(128)} %tiles_ref.1, bf16[128,1024]{1,0:T(8,128)(2,1)} %q_ref.1, bf16[128,1024]{1,0:T(8,128)(2,1)} %g_ref.1, f32[1,128]{1,0:T(1,128)} %bitcast.1, ...), custom_call_target="tpu_custom_call" | custom-call | tf_op jit(solution)/shard_map/attention/pallas_call | solution.py:498
  82.4 3.3 %hand_over.1 = (bf16[16,8192]{1,0:T(8,128)(2,1)}, bf16[1,6404,128]{2,1,0:T(8,128)(2,1)}, bf16[1,6404,128]{2,1,0:T(8,128)(2,1)}) custom-call(bf16[16,8192]{1,0:T(8,128)(2,1)} %get-tuple-element.6.text_in, bf16[1,6404,128]{2,1,0:T(8,128)(2,1)} %get-tuple-element.7.key_in, bf16[1,6404,128]{2,1,0:T(8,128)(2,1)} %get-tuple-element.8.value_in), custom_call_target="tpu_custom_call" | custom-call | tf_op jit(solution)/shard_map/hand_over/pallas_call | solution.py:551

commit v4 on v3

--- a/solution.py
+++ b/solution.py
@@ -91,6 +91,8 @@
     padded = keys.shape[0]
     chunks = padded // CHUNK
     groups = cols // GROUP
+    own_totals = chunks * 2 // 3
+    own_grads = chunks // 4
     limit = jnp.int32(0)
     for i in range(slot_ref.shape[0]):
         limit += jnp.where(slot_ref[i] == seq, tiles_ref[i], 0)
@@ -152,6 +154,9 @@
         normed = raw * inv * gain
         qt[0, :, span] = normed.T.astype(bf16)
 
+    rest = slice(own_grads * CHUNK, padded)
+    dkt[:, rest] = jnp.zeros_like(dkt[:, rest])
+    dvt[:, rest] = jnp.zeros_like(dvt[:, rest])
     pl.semaphore_wait(barrier, 5)
 
     @pl.when(has_left)
@@ -200,22 +205,31 @@
     def chunk_start(i):
         return pl.multiple_of(i * CHUNK, CHUNK)
 
-    def totals_pass(b, stats):
+    def totals_pass(b, stats, low_chunk, high_chunk, fills=0):
         def scores_of(start, j):
             return nn(keys[pl.ds(start, CHUNK), :], qt[b, :, columns(j)])
 
         for j in range(groups):
-            first = scores_of(0, j)
-            held[:, columns(j)] = first
-            stats[0:1, columns(j)] = jnp.max(first, axis=0, keepdims=True) * exp2_scale
-        stats[1:2, :] = stats[0:1, :]
-        acc[...] = jnp.zeros_like(acc)
-
-        def step(i, carry, last=False):
+            span = columns(j)
+            first = scores_of(low_chunk * CHUNK, j)
+            held[:, span] = first
+            top = jnp.max(first, axis=0, keepdims=True) * exp2_scale
+            if low_chunk == 0:
+                stats[0:1, span] = top
+                stats[1:2, span] = top
+            else:
+                before = stats[0:1, span]
+                stats[0:1, span] = jnp.maximum(before, top)
+                stats[1:2, span] = before
+        if low_chunk == 0:
+            acc[b] = jnp.zeros(acc.shape[1:], f32)
+
+        def step(i, carry, last=False, fill=False):
             start = chunk_start(i)
             value_chunk = values_t[:, pl.ds(start, CHUNK)]
-            if b == 0 and not last:
-                fill_chunk(jnp.minimum(i + 2, whole - 1))
+            if fill:
+                fill_chunk(2 * i + 2)
+                fill_chunk(2 * i + 3)
             for j in range(groups):
                 span = columns(j)
                 top = stats[0:1, span]
@@ -230,31 +244,34 @@
                         top, jnp.max(later, axis=0, keepdims=True) * exp2_scale
                     )
                     stats[1:2, span] = top
-                acc[:, span] = acc[:, span] * jnp.exp2(before - top) + nn(value_chunk, low)
+                acc[b, :, span] = acc[b, :, span] * jnp.exp2(before - top) + nn(value_chunk, low)
             return carry
 
-        lax.fori_loop(0, chunks - 1, step, 0)
-        step(chunks - 1, 0, True)
-        stats[1:2, :] = acc[HD : HD + 1, :]
+        if fills:
+            lax.fori_loop(low_chunk, fills, functools.partial(step, fill=True), 0)
+        lax.fori_loop(max(low_chunk, fills), high_chunk - 1, step, 0)
+        step(high_chunk - 1, 0, last=True)
 
     def finish_totals(b, stats):
-        stats[2:3, :] = jnp.sum(acc[0:HD, :] * gt[b].astype(f32), axis=0, keepdims=True)
-
-    totals_pass(0, stats_own)
+        stats[1:2, :] = acc[b, HD : HD + 1, :]
+        stats[2:3, :] = jnp.sum(acc[b, 0:HD, :] * gt[b].astype(f32), axis=0, keepdims=True)
+
+    totals_pass(0, stats_own, 0, own_totals, fills=(whole - 2) // 2)
 
     @pl.when(has_left)
     def _():
         g_copy.start()
 
-    finish_totals(0, stats_own)
-
     @pl.when(has_next)
     def _():
         q_copy.wait_recv()
-        totals_pass(1, stats_send)
+        totals_pass(1, stats_send, 0, chunks)
         g_copy.wait_recv()
         finish_totals(1, stats_send)
         stats_copy.start()
+
+    totals_pass(0, stats_own, own_totals, chunks)
+    finish_totals(0, stats_own)
 
     @pl.when(has_left)
     def _():
@@ -274,13 +291,14 @@
         total[0, 0:1, :] = stats_own[0:1, :] + jnp.log2(norm)
         total[0, 1:2, :] = stats_own[2:3, :] / norm
 
-    def grads_pass(b, totals, write):
+    def grads_pass(b, totals, write, low_chunk, high_chunk):
         def slopes_of(start, j):
             return nn(values[pl.ds(start, CHUNK), :], gt[b, :, columns(j)])
 
         for j in range(groups):
-            held[:, columns(j)] = slopes_of(0, j)
-        dqt[...] = jnp.zeros_like(dqt)
+            held[:, columns(j)] = slopes_of(low_chunk * CHUNK, j)
+        if low_chunk == 0:
+            dqt[b] = jnp.zeros(dqt.shape[1:], f32)
 
         def step(i, carry, last=False):
             start = chunk_start(i)
@@ -298,14 +316,14 @@
                 grads_t[span, :] = score_grad.T
                 v_part = nn(gt[b, :, span], probs_t[span, :])
                 k_part = nn(qt[b, :, span], grads_t[span, :])
-                dqt[:, span] += nn(key_chunk, score_grad)
+                dqt[b, :, span] += nn(key_chunk, score_grad)
                 key_part = k_part if j == 0 else key_part + k_part
                 value_part = v_part if j == 0 else value_part + v_part
             write(start, key_part, value_part)
             return carry
 
-        lax.fori_loop(0, chunks - 1, step, 0)
-        step(chunks - 1, 0, True)
+        lax.fori_loop(low_chunk, high_chunk - 1, step, 0)
+        step(high_chunk - 1, 0, True)
 
     def hold(start, key_part, value_part):
         dkt[:, pl.ds(start, CHUNK)] = key_part
@@ -314,20 +332,17 @@
     def emit(start, key_part, value_part):
         hold(start, key_part + dkt[:, pl.ds(start, CHUNK)], value_part + dvt[:, pl.ds(start, CHUNK)])
 
+    grads_pass(0, total.at[0], hold, 0, own_grads)
+
     @pl.when(has_next)
     def _():
         total_copy.wait_recv()
-        grads_pass(1, total_in, hold)
-        dq_send[...] = dqt[...].astype(bf16)
+        grads_pass(1, total_in, emit, 0, chunks)
+        dq_send[...] = dqt[1].astype(bf16)
         dq_copy.start()
 
-    @pl.when(jnp.logical_not(has_next))
-    def _():
-        dkt[...] = jnp.zeros_like(dkt)
-        dvt[...] = jnp.zeros_like(dvt)
-
     weight_copies[0].start()
-    grads_pass(0, total.at[0], emit)
+    grads_pass(0, total.at[0], emit, own_grads, chunks)
 
     def output(i):
         start = i * CHUNK
@@ -345,13 +360,13 @@
     @pl.when(has_left)
     def _():
         dq_copy.wait_recv()
-        dqt[...] += dq_in[...].astype(f32)
+        dqt[0] += dq_in[...].astype(f32)
 
     for h in range(heads):
         span = slice(h * HD, (h + 1) * HD)
         raw = q_ref[:, span].astype(f32)
         inv = lax.rsqrt(jnp.mean(raw * raw, axis=-1, keepdims=True) + norm_eps)
-        scaled = dqt[:, span].T * score_scale * gain
+        scaled = dqt[0, :, span].T * score_scale * gain
         spread = jnp.mean(scaled * raw, axis=-1, keepdims=True)
         raw_low[:, span] = (inv * scaled - raw * (inv * inv * inv) * spread).astype(bf16)
 
@@ -518,10 +533,10 @@
             V((CHUNK, cols), f32),
             V((cols, CHUNK), bf16),
             V((cols, CHUNK), bf16),
-            V((HD + 16, cols), f32),
+            V((2, HD + 16, cols), f32),
             V((HD, padded), f32),
             V((HD, padded), f32),
-            V((HD, cols), f32),
+            V((2, HD, cols), f32),
             V((8, cols), f32),
             V((8, cols), f32),
             V((8, cols), f32),

time: 86 us -> 80.1 us (0.931)
  Pallas kernels: 85.1 us -> 79.2 us
    pallas_call x1, Pallas kernels: 81.8 us -> 75.9 us  [on_device(): pl.pallas_call(attention_kernel, out_shape=(jax.ShapeDtypeStruct((rows //...]
where the time goes in v4:
time: 80.1 us; the launch traced here: 80 us
  Pallas kernels  79.2 us (99%)
    pallas_call x1, Pallas kernels, on_device(): pl.pallas_call(attention_kernel, out_shape=(jax.ShapeDtypeStruct((rows //...  75.9 us
    pallas_call x1, Pallas kernels, on_device(): pl.pallas_call(hand_over_kernel, out_shape=tuple((jax.ShapeDtypeStruct(x....  3.33 us

profile of v4, /device:TPU:0, one launch (start us, length us, event | category | flops | bytes accessed | tf_op | source)
XLA Modules:
  0.0 80.0 jit_solution(3768286001679457395)
XLA Ops:
  0.6 75.9 %attention.1 = (bf16[16,8192]{1,0:T(8,128)(2,1)}, bf16[1,6404,128]{2,1,0:T(8,128)(2,1)}, bf16[1,6404,128]{2,1,0:T(8,128)(2,1)}) custom-call(s32[16]{0:T(128)} %slot_ref.1, s32[16]{0:T(128)} %tiles_ref.1, bf16[128,1024]{1,0:T(8,128)(2,1)} %q_ref.1, bf16[128,1024]{1,0:T(8,128)(2,1)} %g_ref.1, f32[1,128]{1,0:T(1,128)} %bitcast.1, ...), custom_call_target="tpu_custom_call" | custom-call | tf_op jit(solution)/shard_map/attention/pallas_call | solution.py:513
  76.5 3.3 %hand_over.1 = (bf16[16,8192]{1,0:T(8,128)(2,1)}, bf16[1,6404,128]{2,1,0:T(8,128)(2,1)}, bf16[1,6404,128]{2,1,0:T(8,128)(2,1)}) custom-call(bf16[16,8192]{1,0:T(8,128)(2,1)} %get-tuple-element.6.text_in, bf16[1,6404,128]{2,1,0:T(8,128)(2,1)} %get-tuple-element.7.key_in, bf16[1,6404,128]{2,1,0:T(8,128)(2,1)} %get-tuple-element.8.value_in), custom_call_target="tpu_custom_call" | custom-call | tf_op jit(solution)/shard_map/hand_over/pallas_call | solution.py:566

commit v5 on v4

--- a/solution.py
+++ b/solution.py
@@ -13,6 +13,7 @@
 CHUNK = 512
 GROUP = 256
 PARTS = 8
+UNROLL = 4
 norm_eps = 1e-05
 score_scale = 1.0 / math.sqrt(HD)
 exp2_scale = score_scale * math.log2(math.e)
@@ -26,6 +27,19 @@
 
 def nt(a, b):
     return lax.dot_general(a, b, (((1,), (1,)), ((), ())), preferred_element_type=f32)
+
+
+def run_chunks(unroll, low, high, step):
+    trips = (high - low) // unroll
+
+    def body(k, carry):
+        for u in range(unroll):
+            step(low + k * unroll + u, 0)
+        return carry
+
+    lax.fori_loop(0, trips, body, 0)
+    for i in range(low + trips * unroll, high):
+        step(i, 0)
 
 
 def attention_kernel(
@@ -154,18 +168,12 @@
         normed = raw * inv * gain
         qt[0, :, span] = normed.T.astype(bf16)
 
-    rest = slice(own_grads * CHUNK, padded)
-    dkt[:, rest] = jnp.zeros_like(dkt[:, rest])
-    dvt[:, rest] = jnp.zeros_like(dvt[:, rest])
     pl.semaphore_wait(barrier, 5)
 
     @pl.when(has_left)
     def _():
         q_copy.start()
 
-    for h in range(heads):
-        span = slice(h * HD, (h + 1) * HD)
-        gt[0, :, span] = g_ref[:, span].T
     for copy in row_copies:
         copy.wait()
     first_key = key_rows_ref[0:1, :]
@@ -248,8 +256,8 @@
             return carry
 
         if fills:
-            lax.fori_loop(low_chunk, fills, functools.partial(step, fill=True), 0)
-        lax.fori_loop(max(low_chunk, fills), high_chunk - 1, step, 0)
+            run_chunks(1, low_chunk, fills, functools.partial(step, fill=True))
+        run_chunks(UNROLL, max(low_chunk, fills), high_chunk - 1, step)
         step(high_chunk - 1, 0, last=True)
 
     def finish_totals(b, stats):
@@ -257,6 +265,12 @@
         stats[2:3, :] = jnp.sum(acc[b, 0:HD, :] * gt[b].astype(f32), axis=0, keepdims=True)
 
     totals_pass(0, stats_own, 0, own_totals, fills=(whole - 2) // 2)
+    for h in range(heads):
+        span = slice(h * HD, (h + 1) * HD)
+        gt[0, :, span] = g_ref[:, span].T
+    rest = slice(own_grads * CHUNK, padded)
+    dkt[:, rest] = jnp.zeros_like(dkt[:, rest])
+    dvt[...] = jnp.zeros_like(dvt)
 
     @pl.when(has_left)
     def _():
@@ -312,25 +326,30 @@
                 score_grad = (probs * (held[:, span] - totals[1:2, span])).astype(bf16)
                 if not last:
                     held[:, span] = slopes_of(chunk_start(i + 1), j)
-                probs_t[span, :] = probs_low.T
+                if b == 0:
+                    e_all[b, pl.ds(start, CHUNK), span] = probs_low
+                else:
+                    probs_t[span, :] = probs_low.T
                 grads_t[span, :] = score_grad.T
-                v_part = nn(gt[b, :, span], probs_t[span, :])
                 k_part = nn(qt[b, :, span], grads_t[span, :])
                 dqt[b, :, span] += nn(key_chunk, score_grad)
                 key_part = k_part if j == 0 else key_part + k_part
-                value_part = v_part if j == 0 else value_part + v_part
+                if b > 0:
+                    v_part = nn(gt[b, :, span], probs_t[span, :])
+                    value_part = v_part if j == 0 else value_part + v_part
             write(start, key_part, value_part)
             return carry
 
-        lax.fori_loop(low_chunk, high_chunk - 1, step, 0)
+        run_chunks(UNROLL, low_chunk, high_chunk - 1, step)
         step(high_chunk - 1, 0, True)
 
     def hold(start, key_part, value_part):
         dkt[:, pl.ds(start, CHUNK)] = key_part
-        dvt[:, pl.ds(start, CHUNK)] = value_part
 
     def emit(start, key_part, value_part):
-        hold(start, key_part + dkt[:, pl.ds(start, CHUNK)], value_part + dvt[:, pl.ds(start, CHUNK)])
+        dkt[:, pl.ds(start, CHUNK)] += key_part
+        if value_part is not None:
+            dvt[:, pl.ds(start, CHUNK)] += value_part
 
     grads_pass(0, total.at[0], hold, 0, own_grads)
 
@@ -350,7 +369,7 @@
         live = start + lax.broadcasted_iota(jnp.int32, (rows, HD), 0) < limit
         span = slice(start, start + CHUNK)
         key_rows = (dkt[:, span] * score_scale).T[0:rows]
-        value_rows = dvt[:, span].T[0:rows]
+        value_rows = (dvt[:, span] + nt(gt[0], e_all[0, span, :])).T[0:rows]
         key_rows_ref[start : start + rows, :] = jnp.where(live, key_rows, 0.0).astype(bf16)
         value_rows_ref[start : start + rows, :] = jnp.where(live, value_rows, 0.0).astype(bf16)
         if i == chunks - 1:
@@ -559,7 +578,7 @@
             pltpu.SemaphoreType.DMA((5, PARTS)),
         ],
         compiler_params=pltpu.CompilerParams(
-            collective_id=0, has_side_effects=True, vmem_limit_bytes=63 << 20
+            collective_id=0, has_side_effects=True, vmem_limit_bytes=255 << 18
         ),
         name="attention",
     )(image_slot, tile_counts, q_raw, out_grad, q_gain.reshape(1, HD), image_keys, image_values, q_weight)

time: 80.1 us -> 77.8 us (0.971)
  Pallas kernels: 79.2 us -> 76.8 us
    pallas_call x1, Pallas kernels: 75.9 us -> 73.5 us  [on_device(): pl.pallas_call(attention_kernel, out_shape=(jax.ShapeDtypeStruct((rows //...]
where the time goes in v5:
time: 77.8 us; the launch traced here: 77.6 us
  Pallas kernels  76.8 us (99%)
  between operations  0.82 us (1%)
    pallas_call x1, Pallas kernels, on_device(): pl.pallas_call(attention_kernel, out_shape=(jax.ShapeDtypeStruct((rows //...  73.5 us
    pallas_call x1, Pallas kernels, on_device(): pl.pallas_call(hand_over_kernel, out_shape=tuple((jax.ShapeDtypeStruct(x....  3.33 us

profile of v5, /device:TPU:0, one launch (start us, length us, event | category | flops | bytes accessed | tf_op | source)
XLA Modules:
  0.0 77.6 jit_solution(7181173939549579066)
XLA Ops:
  0.6 73.5 %attention.1 = (bf16[16,8192]{1,0:T(8,128)(2,1)}, bf16[1,6404,128]{2,1,0:T(8,128)(2,1)}, bf16[1,6404,128]{2,1,0:T(8,128)(2,1)}) custom-call(s32[16]{0:T(128)} %slot_ref.1, s32[16]{0:T(128)} %tiles_ref.1, bf16[128,1024]{1,0:T(8,128)(2,1)} %q_ref.1, bf16[128,1024]{1,0:T(8,128)(2,1)} %g_ref.1, f32[1,128]{1,0:T(1,128)} %bitcast.1, ...), custom_call_target="tpu_custom_call" | custom-call | tf_op jit(solution)/shard_map/attention/pallas_call | solution.py:532
  74.1 3.3 %hand_over.1 = (bf16[16,8192]{1,0:T(8,128)(2,1)}, bf16[1,6404,128]{2,1,0:T(8,128)(2,1)}, bf16[1,6404,128]{2,1,0:T(8,128)(2,1)}) custom-call(bf16[16,8192]{1,0:T(8,128)(2,1)} %get-tuple-element.6.text_in, bf16[1,6404,128]{2,1,0:T(8,128)(2,1)} %get-tuple-element.7.key_in, bf16[1,6404,128]{2,1,0:T(8,128)(2,1)} %get-tuple-element.8.value_in), custom_call_target="tpu_custom_call" | custom-call | tf_op jit(solution)/shard_map/hand_over/pallas_call | solution.py:585

commit v6 on v5

--- a/solution.py
+++ b/solution.py
@@ -466,8 +466,8 @@
         for lag, stage in ((0, multiply), (3, send_far), (6, send_near), (10, finish)):
             if 0 <= t - lag < PARTS:
                 stage(t - lag)
-        if 3 <= t < chunks + 3:
-            output(t - 3)
+        if 5 <= t < chunks + 5:
+            output(t - 5)
     for copy in out_copies:
         copy.wait()
     for n in range(PARTS):

time: 77.8 us -> 79.2 us (1.018)
  Pallas kernels: 76.8 us -> 78 us
    pallas_call x1, Pallas kernels: 73.5 us -> 74.6 us  [on_device(): pl.pallas_call(attention_kernel, out_shape=(jax.ShapeDtypeStruct((rows //...]
where the time goes in v6:
time: 79.2 us; the launch traced here: 78.8 us
  Pallas kernels  78 us (98%)
  between operations  0.82 us (1%)
    pallas_call x1, Pallas kernels, on_device(): pl.pallas_call(attention_kernel, out_shape=(jax.ShapeDtypeStruct((rows //...  74.6 us
    pallas_call x1, Pallas kernels, on_device(): pl.pallas_call(hand_over_kernel, out_shape=tuple((jax.ShapeDtypeStruct(x....  3.33 us

profile of v6, /device:TPU:0, one launch (start us, length us, event | category | flops | bytes accessed | tf_op | source)
XLA Modules:
  0.0 78.8 jit_solution(5303403177760386279)
XLA Ops:
  0.6 74.6 %attention.1 = (bf16[16,8192]{1,0:T(8,128)(2,1)}, bf16[1,6404,128]{2,1,0:T(8,128)(2,1)}, bf16[1,6404,128]{2,1,0:T(8,128)(2,1)}) custom-call(s32[16]{0:T(128)} %slot_ref.1, s32[16]{0:T(128)} %tiles_ref.1, bf16[128,1024]{1,0:T(8,128)(2,1)} %q_ref.1, bf16[128,1024]{1,0:T(8,128)(2,1)} %g_ref.1, f32[1,128]{1,0:T(1,128)} %bitcast.1, ...), custom_call_target="tpu_custom_call" | custom-call | tf_op jit(solution)/shard_map/attention/pallas_call | solution.py:532
  75.3 3.3 %hand_over.1 = (bf16[16,8192]{1,0:T(8,128)(2,1)}, bf16[1,6404,128]{2,1,0:T(8,128)(2,1)}, bf16[1,6404,128]{2,1,0:T(8,128)(2,1)}) custom-call(bf16[16,8192]{1,0:T(8,128)(2,1)} %get-tuple-element.6.text_in, bf16[1,6404,128]{2,1,0:T(8,128)(2,1)} %get-tuple-element.7.key_in, bf16[1,6404,128]{2,1,0:T(8,128)(2,1)} %get-tuple-element.8.value_in), custom_call_target="tpu_custom_call" | custom-call | tf_op jit(solution)/shard_map/hand_over/pallas_call | solution.py:585
